TPU v7x, 32 devices: a whole 2x2x4 slice. The times are simulated.
32 devices in a mesh: gx: 4 (over y, x), gy: 2 (over core), sa: 4 (over z).
Axes of the slice: x: 2, y: 2, z: 4, core: 2. Of those that a mesh axis runs over, the one named last changes fastest.
Arguments:
- pixels: bfloat16 [16, 512, 8192], P('sa', 'gy', 'gx'), may hold values from -6 to 6
- peak_offsets: int32 [16, 2, 8, 128], P('sa', None, 'gy', 'gx'), may hold values from -2 to 2
- validity: int32 [16, 8, 128], P('sa', 'gy', 'gx'), may hold values 0 or 1
Outputs:
- flow_field: float32 [16, 2, 8, 128], P('sa', None, 'gy', 'gx')
- mesh_field: float32 [16, 2, 8, 128], P('sa', None, 'gy', 'gx')
All inputs are finite; a program needn't handle non-finite values. No bound on the sum of `validity` on one device may be relied on, other than what follows from the above.
Results may differ from a plain program's by a relative error of at most 0.0035.
Values may be sent and summed in bfloat16 or wider, within the bound.
A program may use at most 192 MiB of HBM per device.

v0:
```python
import math

import jax
import jax.numpy as jnp
from jax import lax
from jax.sharding import PartitionSpec as P

PATCH = 64
RELAX = 8


spring_plane = 0.5
spring_stack = 1.0
step_size = 0.2
damping = 0.6
whiten_floor = 1024.0


def shifted(block, axis, distance):
    devices = range(lax.axis_size(axis))
    route = [(i - distance, i) for i in devices if i - distance in devices]
    return lax.ppermute(block, axis, route)


def dft_tables():
    frequency = jnp.arange(PATCH, dtype=jnp.int32)
    phases = frequency[:, None] * frequency[None, :] % PATCH
    angles = phases.astype(jnp.float32) * (2.0 * math.pi / PATCH)
    return (jnp.cos(angles).astype(jnp.bfloat16), jnp.sin(angles).astype(jnp.bfloat16))


def column_tables():
    position = jnp.arange(2 * PATCH, dtype=jnp.int32)
    same_block = position[:, None] // PATCH == position[None, :] // PATCH
    phases = position[:, None] % PATCH * (position[None, :] % PATCH) % PATCH
    angles = phases.astype(jnp.float32) * (2.0 * math.pi / PATCH)
    cosine = jnp.where(same_block, jnp.cos(angles).astype(jnp.bfloat16).astype(jnp.float32), 0.0)
    sine_table = jnp.where(
        same_block, jnp.sin(angles).astype(jnp.bfloat16).astype(jnp.float32), 0.0
    )
    return (cosine.astype(jnp.bfloat16), (-sine_table).astype(jnp.bfloat16))


def transform_rows(row_table, blocks):
    return jnp.einsum("kx,axc->akc", row_table, blocks, preferred_element_type=jnp.float32)


def spectra(section_image):
    height, breadth = section_image.shape
    cosine_cols, sine_cols = column_tables()
    flat = section_image.reshape(-1, 2 * PATCH)
    col_real = (
        jnp.dot(flat, cosine_cols, preferred_element_type=jnp.float32)
        .astype(jnp.bfloat16)
        .reshape(height // PATCH, PATCH, breadth)
    )
    col_imag = (
        jnp.dot(flat, sine_cols, preferred_element_type=jnp.float32)
        .astype(jnp.bfloat16)
        .reshape(height // PATCH, PATCH, breadth)
    )
    cosine, sine_table = dft_tables()
    spec_real = transform_rows(cosine, col_real) + transform_rows(sine_table, col_imag)
    spec_imag = transform_rows(cosine, col_imag) - transform_rows(sine_table, col_real)
    return (
        spec_real.reshape(height, breadth).astype(jnp.bfloat16),
        spec_imag.reshape(height, breadth).astype(jnp.bfloat16),
    )


def phase_tables(offsets):
    frequency = jnp.arange(PATCH, dtype=jnp.int32)
    nearby = jnp.arange(3, dtype=jnp.int32) - 1
    phases = (
        frequency[None, None, :, None]
        * (offsets[:, :, None, None] + nearby[None, None, None, :])
        % PATCH
    )
    angles = phases.astype(jnp.float32) * (2.0 * math.pi / PATCH)
    return (jnp.cos(angles).astype(jnp.bfloat16), jnp.sin(angles).astype(jnp.bfloat16))


def subpixel(correlation, offsets):
    center = correlation[..., 1, 1]
    row_low = correlation[..., 0, 1]
    row_high = correlation[..., 2, 1]
    col_low = correlation[..., 1, 0]
    col_high = correlation[..., 1, 2]
    row_step = (row_low - row_high) / (
        2.0 * jnp.maximum(jnp.abs(row_low - 2.0 * center + row_high), 1.0)
    )
    col_step = (col_low - col_high) / (
        2.0 * jnp.maximum(jnp.abs(col_low - 2.0 * center + col_high), 1.0)
    )
    return jnp.stack(
        [offsets[0].astype(jnp.float32) + row_step, offsets[1].astype(jnp.float32) + col_step], 0
    )


def refine(current, previous, offsets):
    patch_rows, patch_cols = (offsets.shape[1], offsets.shape[2])
    layout = (patch_rows, PATCH, patch_cols, PATCH)
    now_real = current[0].astype(jnp.float32).reshape(layout)
    now_imag = current[1].astype(jnp.float32).reshape(layout)
    old_real = previous[0].astype(jnp.float32).reshape(layout)
    old_imag = previous[1].astype(jnp.float32).reshape(layout)
    cross_real = now_real * old_real + now_imag * old_imag
    cross_imag = now_imag * old_real - now_real * old_imag
    scale = jnp.sqrt(
        cross_real * cross_real + cross_imag * cross_imag + whiten_floor * whiten_floor
    )
    prod_real = (cross_real / scale).astype(jnp.bfloat16)
    prod_imag = (cross_imag / scale).astype(jnp.bfloat16)
    col_cos, col_sin = phase_tables(offsets[1])
    row_cos, row_sin = phase_tables(offsets[0])
    wide = jnp.float32
    half_real = (
        jnp.einsum("akbj,abjd->akbd", prod_real, col_cos, preferred_element_type=wide)
        - jnp.einsum("akbj,abjd->akbd", prod_imag, col_sin, preferred_element_type=wide)
    ).astype(jnp.bfloat16)
    half_imag = (
        jnp.einsum("akbj,abjd->akbd", prod_real, col_sin, preferred_element_type=wide)
        + jnp.einsum("akbj,abjd->akbd", prod_imag, col_cos, preferred_element_type=wide)
    ).astype(jnp.bfloat16)
    correlation = (
        jnp.einsum("akbd,abke->abed", half_real, row_cos, preferred_element_type=wide)
        - jnp.einsum("akbd,abke->abed", half_imag, row_sin, preferred_element_type=wide)
    ) / float(PATCH)
    return subpixel(correlation, offsets)


def edge_degree(row_index, col_index, total_rows, total_cols):
    return (
        4.0
        - (row_index == 0).astype(jnp.float32)
        - (row_index == total_rows - 1).astype(jnp.float32)
        - (col_index == 0).astype(jnp.float32)
        - (col_index == total_cols - 1).astype(jnp.float32)
    )


def spring_step(state, velocity, padded, weight, flow_field, weight_next, flow_next, degree):
    neighbours = (
        padded[1:-1, :, :-2, 1:-1]
        + padded[1:-1, :, 2:, 1:-1]
        + padded[1:-1, :, 1:-1, :-2]
        + padded[1:-1, :, 1:-1, 2:]
    )
    lower_mesh = padded[:-2, :, 1:-1, 1:-1]
    upper_mesh = padded[2:, :, 1:-1, 1:-1]
    here_term = weight * (state - lower_mesh - flow_field)
    next_term = weight_next * (upper_mesh - state - flow_next)
    gradient = spring_plane * (degree * state - neighbours) + spring_stack * (here_term - next_term)
    velocity = damping * velocity - step_size * gradient
    return (state + velocity, velocity)


def arrange_whole(gathered, count_x, count_y, count_s):
    shape = gathered.shape
    blocks = gathered.reshape((count_x, count_y, count_s) + shape[1:])
    blocks = jnp.transpose(blocks, (2, 3, 4, 1, 5, 0, 6))
    return blocks.reshape(count_s * shape[1], shape[2], count_y * shape[3], count_x * shape[4])


def per_device(pixels, peak_offsets, validity):
    count = pixels.shape[0]
    last_spectra = None
    last_spectra = spectra(pixels[count - 1])
    earlier = shifted((last_spectra[0], last_spectra[1]), "sa", 1)
    flows = []
    for section in range(count):
        if last_spectra is not None and section == count - 1:
            current = last_spectra
        else:
            current = spectra(pixels[section])
        flows.append(refine(current, earlier, peak_offsets[section]))
        earlier = current
    flow_field = jnp.stack(flows, 0)
    weight = validity.astype(jnp.float32)[:, None]
    patch_rows, patch_cols = (flow_field.shape[2], flow_field.shape[3])
    count_x, count_y, count_s = (lax.axis_size("gx"), lax.axis_size("gy"), lax.axis_size("sa"))
    total_rows = patch_rows * count_y
    total_cols = patch_cols * count_x
    whole_flow, whole_weight = (
        lax.all_gather(flow_field[None], ("gx", "gy", "sa"), axis=0, tiled=True),
        lax.all_gather(weight[None], ("gx", "gy", "sa"), axis=0, tiled=True),
    )
    all_flow = arrange_whole(whole_flow, count_x, count_y, count_s)
    all_weight = arrange_whole(whole_weight, count_x, count_y, count_s)
    all_state = jnp.cumsum(all_flow, axis=0)
    weight_next = jnp.concatenate([all_weight[1:], jnp.zeros_like(all_weight[:1])], 0)
    flow_next = jnp.concatenate([all_flow[1:], jnp.zeros_like(all_flow[:1])], 0)
    row_index = jnp.arange(total_rows, dtype=jnp.int32)[:, None]
    col_index = jnp.arange(total_cols, dtype=jnp.int32)[None, :]
    degree = edge_degree(row_index, col_index, total_rows, total_cols)

    def relax_whole(carry, unused):
        state, velocity = carry
        padded = jnp.pad(state, ((1, 1), (0, 0), (1, 1), (1, 1)))
        return (
            spring_step(
                state, velocity, padded, all_weight, all_flow, weight_next, flow_next, degree
            ),
            None,
        )

    final, unused_out = lax.scan(
        relax_whole, (all_state, jnp.zeros_like(all_state)), None, length=RELAX
    )
    zero = jnp.zeros((), jnp.int32)
    starts = (
        lax.axis_index("sa") * count,
        zero,
        lax.axis_index("gy") * patch_rows,
        lax.axis_index("gx") * patch_cols,
    )
    mesh_field = lax.dynamic_slice(final[0], starts, flow_field.shape)
    return (flow_field, mesh_field)


def solution(mesh):
    return jax.shard_map(
        per_device,
        mesh=mesh,
        in_specs=(P("sa", "gy", "gx"), P("sa", None, "gy", "gx"), P("sa", "gy", "gx")),
        out_specs=(P("sa", None, "gy", "gx"), P("sa", None, "gy", "gx")),
        check_vma=False,
    )
```

profile of v0, /device:TPU:0, one launch (start us, length us, event | category | flops | bytes accessed | tf_op | source)
XLA Modules:
  0.0 375.0 jit_solution(17197773067415291159)
XLA Ops:
  0.6 4.0 %fusion.499 = (bf16[1,256,2048]{2,1,0:T(8,128)(2,1)}, bf16[1,256,2048]{2,1,0:T(8,128)(2,1)S(1)}, bf16[1,256,2048]{2,1,0:T(8,128)(2,1)}, bf16[1,256,2048]{2,1,0:T(8,128)(2,1)}) fusion(bf16[4,256,2048]{2,1,0:T(8,128)(2,1)} %param.5), kind=kLoop, calls=%fused_computation.549 | loop fusion | bytes 8388608 | tf_op jit(solution)/shard_map/slice | solution.py:175
  12.6 3.8 %bitcast_convert_fusion.1 = (f32[4,64,2048]{2,1,0:T(8,128)}, bf16[4,2048,64]{1,2,0:T(8,128)(2,1)}) fusion(f32[4,2048,64]{1,2,0:T(8,128)} %fusion.241, bf16[4,64,2048]{2,1,0:T(8,128)(2,1)S(1)} %reshape.869), kind=kOutput, calls=%fused_computation.157 | convolution fusion | flops 68743168 | bytes 6291456 | tf_op jit(solution)/shard_map/kx,axc->akc/dot_general | solution.py:45
  16.4 5.9 %collective-permute-start = (bf16[256,2048]{1,0:T(8,128)(2,1)}, bf16[256,2048]{1,0:T(8,128)(2,1)}, u32[]{:S(2)}, u32[]{:S(2)}) collective-permute-start(bf16[256,2048]{1,0:T(8,128)(2,1)} %bitcast.11), channel_id=1, source_target_pairs={{0,1},{1,2},{2,3},{4,5},{5,6},{6,7},{8,9},{9,10},{10,11},{12,13},{... | collective-permute-start | bytes 3145736 | tf_op jit(solution)/shard_map/ppermute | solution.py:22
  22.9 2.2 bitcast_convert_fusion
  25.1 3.8 %collective-permute-start.1 = (bf16[256,2048]{1,0:T(8,128)(2,1)}, bf16[256,2048]{1,0:T(8,128)(2,1)}, u32[]{:S(2)}, u32[]{:S(2)}) collective-permute-start(bf16[256,2048]{1,0:T(8,128)(2,1)} %bitcast.14), channel_id=1, source_target_pairs={{0,1},{1,2},{2,3},{4,5},{5,6},{6,7},{8,9},{9,10},{10,11},{12,13},{... | collective-permute-start | bytes 3145736 | tf_op jit(solution)/shard_map/ppermute | solution.py:22
  41.2 3.0 reshape.892
  44.2 4.9 %reshape.893 = f32[4,64,32,64]{3,2,1,0:T(8,128)} reshape(f32[4,64,2048]{2,1,0:T(8,128)} %get-tuple-element.239) | data formatting | bytes 4194304 | tf_op jit(solution)/shard_map/convert_element_type | solution.py:104
  53.3 1.9 fusion.249
  57.1 4.9 %reshape.888 = f32[4,64,32,64]{3,2,1,0:T(8,128)} reshape(f32[4,64,2048]{2,1,0:T(8,128)} %fusion.35) | data formatting | bytes 4194304 | tf_op jit(solution)/shard_map/convert_element_type | solution.py:103
  62.0 2.1 fusion.38
  64.2 3.0 reshape.889
  75.7 4.9 %reshape.890 = f32[4,64,32,64]{3,2,1,0:T(8,128)} reshape(f32[4,64,2048]{2,1,0:T(8,128)} %fusion.41) | data formatting | bytes 4194304 | tf_op jit(solution)/shard_map/convert_element_type | solution.py:103
  80.5 2.1 fusion.44
  82.7 3.0 reshape.891
  86.9 1.9 fusion.239
  93.8 4.8 %reshape.882 = f32[4,64,32,64]{3,2,1,0:T(8,128)} reshape(f32[4,64,2048]{2,1,0:T(8,128)} %fusion.27) | data formatting | bytes 4194304 | tf_op jit(solution)/shard_map/convert_element_type | solution.py:103
  98.6 2.1 fusion.31
  100.8 3.1 reshape.885
  103.9 66.2 %all-gather.1 = f32[128,4,32]{2,1,0:T(4,128)S(1)} all-gather(f32[4,4,32]{2,1,0:T(4,128)S(1)} %convert_element_type.775), channel_id=3, replica_groups=mesh['gx'=4,'gy'=2,'sa'=4] {'gx','gy','sa'}, dimensions={0}, use_global_device_ids=true | all-gather | bytes 67584 | tf_op jit(solution)/shard_map/all_gather | solution.py:186
  170.7 4.7 %reshape.884 = f32[4,64,32,64]{3,2,1,0:T(8,128)} reshape(bf16[256,2048]{1,0:T(8,128)(2,1)} %collective-permute-done) | data formatting | bytes 3145728 | tf_op jit(solution)/shard_map/reshape | solution.py:105
  175.4 4.5 %reshape.887 = f32[4,64,32,64]{3,2,1,0:T(8,128)} reshape(bf16[256,2048]{1,0:T(8,128)(2,1)} %collective-permute-done.1) | data formatting | bytes 3145728 | tf_op jit(solution)/shard_map/reshape | solution.py:106
  179.9 27.3 %divide_convert_fusion.7 = (bf16[4,64,32,64]{3,2,1,0:T(8,128)(2,1)}, f32[4,64,32,64]{3,2,1,0:T(8,128)}, f32[4,64,32,64]{3,2,1,0:T(8,128)}, bf16[4,64,32,64]{3,2,...) fusion(f32[4,64,32,64]{3,2,1,0:T(8,128)} %reshape.885, ...), kind=kLoop, calls=%fused_computation.56 | loop fusion | flops 25165824 | bytes 41943040 | tf_op jit(solution)/shard_map/convert_element_type | solution.py:112
  207.2 5.4 %divide_convert_fusion.2 = bf16[4,64,32,64]{3,2,1,0:T(8,128)(2,1)S(1)} fusion(f32[4,64,32,64]{3,2,1,0:T(8,128)} %get-tuple-element.200, f32[4,64,32,64]{3,2,1,0:T(8,128)} %get-tuple-element.201), kind=kLoop, calls=%fused_computation.45 | loop fusion | flops 3145728 | bytes 5242880 | tf_op jit(solution)/shard_map/convert_element_type | solution.py:113
  212.6 3.4 fusion.53
  216.0 3.7 fusion.55
  219.7 1.9 divide_convert_fusion.6
  221.6 2.7 fusion.69
  224.3 3.4 fusion.71
  227.7 1.9 divide_convert_fusion
  229.6 2.7 fusion.45
  232.3 2.7 fusion.47
  235.0 1.9 divide_convert_fusion.4
  236.9 2.7 fusion.63
  239.6 2.8 fusion.61
  242.5 6.0 %fusion.155 = f32[4,32,3,3]{3,2,1,0:T(4,128)S(1)} fusion(f32[4,32,3,64]{3,2,1,0:T(4,128)S(1)} %copy-done.21, bf16[4,64,32,64]{3,2,1,0:T(8,128)(2,1)} %get-tuple-element.199, s32[4,32,3]{2,1,0:T(8,128)S(1)} %get-tuple-element.233, s32[4,32,3]{2,1,0:T(8,128)S(1)} %get-tuple-element.234), kind=kOutput, calls=%fused_computation.151 | convolution fusion | flops 4079616 | bytes 1154560 | tf_op jit(solution)/shard_map/akbd,abke->abed/dot_general | solution.py:126
  248.5 6.1 %fusion.102 = f32[4,32,3,3]{3,2,1,0:T(4,128)S(1)} fusion(f32[4,32,3,3]{3,2,1,0:T(4,128)S(1)} %fusion.155, f32[4,32,3,64]{3,2,1,0:T(4,128)S(1)} %copy-done.20, bf16[4,64,32,64]{3,2,1,0:T(8,128)(2,1)} %get-tuple-element.199, s32[4,32,3]{2,1,0:T(8,128)S(1)} %get-tuple-element.233, s32[4,32,3]{2,1,0:T(8,128)S(1)} %get-tuple-element.234), kind=kOutput, calls=%fused_computation.131 | convolution fusion | flops 4081920 | bytes 1159168 | tf_op jit(solution)/shard_map/akbd,abke->abed/dot_general | solution.py:127
  254.6 2.3 slice_reduce_fusion.7
  256.9 6.2 %fusion.133 = f32[4,32,3,3]{3,2,1,0:T(4,128)S(1)} fusion(f32[4,32,3,64]{3,2,1,0:T(4,128)S(1)} %copy-done.19, bf16[4,64,32,64]{3,2,1,0:T(8,128)(2,1)} %get-tuple-element.184, s32[4,32,3]{2,1,0:T(8,128)S(1)} %get-tuple-element.229, s32[4,32,3]{2,1,0:T(8,128)S(1)} %get-tuple-element.230), kind=kOutput, calls=%fused_computation.145 | convolution fusion | flops 4079616 | bytes 1154560 | tf_op jit(solution)/shard_map/akbd,abke->abed/dot_general | solution.py:126
  263.1 6.0 %fusion.104 = f32[4,32,3,3]{3,2,1,0:T(4,128)S(1)} fusion(f32[4,32,3,3]{3,2,1,0:T(4,128)S(1)} %fusion.133, f32[4,32,3,64]{3,2,1,0:T(4,128)S(1)} %fusion.69, bf16[4,64,32,64]{3,2,1,0:T(8,128)(2,1)} %get-tuple-element.184, s32[4,32,3]{2,1,0:T(8,128)S(1)} %get-tuple-element.229, s32[4,32,3]{2,1,0:T(8,128)S(1)} %get-tuple-element.230), kind=kOutput, calls=%fused_computation.135 | convolution fusion | flops 4081920 | bytes 1159168 | tf_op jit(solution)/shard_map/akbd,abke->abed/dot_general | solution.py:127
  269.1 2.3 slice_reduce_fusion.15
  271.4 6.4 %fusion.166 = f32[4,32,3,3]{3,2,1,0:T(4,128)S(1)} fusion(f32[4,32,3,64]{3,2,1,0:T(4,128)S(1)} %fusion.47, bf16[4,64,32,64]{3,2,1,0:T(8,128)(2,1)} %get-tuple-element.202, s32[4,32,3]{2,1,0:T(8,128)S(1)} %get-tuple-element.235, s32[4,32,3]{2,1,0:T(8,128)S(1)} %get-tuple-element.236), kind=kOutput, calls=%fused_computation.154 | convolution fusion | flops 4079616 | bytes 1154560 | tf_op jit(solution)/shard_map/akbd,abke->abed/dot_general | solution.py:126
  277.8 6.1 %fusion.101 = f32[4,32,3,3]{3,2,1,0:T(4,128)S(1)} fusion(f32[4,32,3,3]{3,2,1,0:T(4,128)S(1)} %fusion.166, f32[4,32,3,64]{3,2,1,0:T(4,128)S(1)} %fusion.45, bf16[4,64,32,64]{3,2,1,0:T(8,128)(2,1)} %get-tuple-element.202, s32[4,32,3]{2,1,0:T(8,128)S(1)} %get-tuple-element.235, s32[4,32,3]{2,1,0:T(8,128)S(1)} %get-tuple-element.236), kind=kOutput, calls=%fused_computation.129 | convolution fusion | flops 4081920 | bytes 1159168 | tf_op jit(solution)/shard_map/akbd,abke->abed/dot_general | solution.py:127
  283.8 2.3 slice_reduce_fusion.3
  286.1 6.2 %fusion.144 = f32[4,32,3,3]{3,2,1,0:T(4,128)S(1)} fusion(f32[4,32,3,64]{3,2,1,0:T(4,128)S(1)} %fusion.63, bf16[4,64,32,64]{3,2,1,0:T(8,128)(2,1)} %get-tuple-element.196, s32[4,32,3]{2,1,0:T(8,128)S(1)} %get-tuple-element.231, s32[4,32,3]{2,1,0:T(8,128)S(1)} %get-tuple-element.232), kind=kOutput, calls=%fused_computation.148 | convolution fusion | flops 4079616 | bytes 1154560 | tf_op jit(solution)/shard_map/akbd,abke->abed/dot_general | solution.py:126
  292.2 6.1 %fusion.103 = f32[4,32,3,3]{3,2,1,0:T(4,128)S(1)} fusion(f32[4,32,3,3]{3,2,1,0:T(4,128)S(1)} %fusion.144, f32[4,32,3,64]{3,2,1,0:T(4,128)S(1)} %fusion.61, bf16[4,64,32,64]{3,2,1,0:T(8,128)(2,1)} %get-tuple-element.196, s32[4,32,3]{2,1,0:T(8,128)S(1)} %get-tuple-element.231, s32[4,32,3]{2,1,0:T(8,128)S(1)} %get-tuple-element.232), kind=kOutput, calls=%fused_computation.133 | convolution fusion | flops 4081920 | bytes 1159168 | tf_op jit(solution)/shard_map/akbd,abke->abed/dot_general | solution.py:127
  298.3 2.3 slice_reduce_fusion.11
  300.7 69.3 %all-gather = f32[128,2,4,32]{3,2,1,0:T(4,128)S(1)} all-gather(f32[4,2,4,32]{3,2,1,0:T(4,128)S(1)} %pad_maximum_fusion), channel_id=2, replica_groups=mesh['gx'=4,'gy'=2,'sa'=4] {'gx','gy','sa'}, dimensions={0}, use_global_device_ids=true | all-gather | bytes 135168 | tf_op jit(solution)/shard_map/all_gather | solution.py:185
  372.0 2.1 while.15
  (132 shorter events, 46.5 us)
Async XLA Ops:
  16.4 154.3 %collective-permute-start = (bf16[256,2048]{1,0:T(8,128)(2,1)}, bf16[256,2048]{1,0:T(8,128)(2,1)}, u32[]{:S(2)}, u32[]{:S(2)}) collective-permute-start(bf16[256,2048]{1,0:T(8,128)(2,1)} %bitcast.11), channel_id=1, source_target_pairs={{0,1},{1,2},{2,3},{4,5},{5,6},{6,7},{8,9},{9,10},{10,11},{12,13},{... | collective-permute-start | bytes 3145736 | tf_op jit(solution)/shard_map/ppermute | solution.py:22
  22.9 6.0 %copy-start.15 = (bf16[1,256,2048]{2,1,0:T(8,128)(2,1)S(1)}, bf16[1,256,2048]{2,1,0:T(8,128)(2,1)}, u32[]{:S(2)}) copy-start(bf16[1,256,2048]{2,1,0:T(8,128)(2,1)} %get-tuple-element.208) | copy-start | bytes 3145732
  25.1 150.3 %collective-permute-start.1 = (bf16[256,2048]{1,0:T(8,128)(2,1)}, bf16[256,2048]{1,0:T(8,128)(2,1)}, u32[]{:S(2)}, u32[]{:S(2)}) collective-permute-start(bf16[256,2048]{1,0:T(8,128)(2,1)} %bitcast.14), channel_id=1, source_target_pairs={{0,1},{1,2},{2,3},{4,5},{5,6},{6,7},{8,9},{9,10},{10,11},{12,13},{... | collective-permute-start | bytes 3145736 | tf_op jit(solution)/shard_map/ppermute | solution.py:22
  29.4 3.6 copy-start.14
  33.5 3.5 copy-start.13
  37.6 3.6 copy-start.3
  44.2 5.0 %copy-start.12 = (bf16[4096,128]{0,1:T(8,128)(2,1)S(1)}, bf16[4096,128]{0,1:T(8,128)(2,1)}, u32[]{:S(2)}) copy-start(bf16[4096,128]{0,1:T(8,128)(2,1)} %fusion.21) | copy-start | bytes 3145732
  50.3 1.8 copy-start.11
  53.3 1.9 copy-start.4
  64.1 3.0 copy-start.10
  68.8 1.9 copy-start.9
  71.9 1.9 copy-start.5
  82.7 3.1 copy-start.8
  86.9 1.9 copy-start.7
  90.0 1.9 copy-start.6
  100.8 3.1 copy-start.18
  100.8 69.7 %copy-start.17 = (s32[4,2,4,32]{3,2,1,0:T(4,128)S(1)}, s32[4,2,4,32]{3,2,1,0:T(4,128)}, u32[]{:S(2)}) copy-start(s32[4,2,4,32]{3,2,1,0:T(4,128)} %param.6) | copy-start | bytes 12292
  212.6 7.1 %copy-start.2 = (f32[4,64,32,64]{3,2,1,0:T(8,128)S(1)}, f32[4,64,32,64]{3,2,1,0:T(8,128)}, u32[]{:S(2)}) copy-start(f32[4,64,32,64]{3,2,1,0:T(8,128)} %get-tuple-element.186) | copy-start | bytes 6291460
  216.0 3.8 %copy-start.1 = (f32[4,64,32,64]{3,2,1,0:T(8,128)S(1)}, f32[4,64,32,64]{3,2,1,0:T(8,128)}, u32[]{:S(2)}) copy-start(f32[4,64,32,64]{3,2,1,0:T(8,128)} %get-tuple-element.185) | copy-start | bytes 6291460
  224.3 3.4 copy-start
  239.6 2.9 copy-start.21
  242.5 6.0 %copy-start.20 = (f32[4,32,3,64]{3,2,1,0:T(4,128)S(1)}, f32[4,32,3,64]{3,2,1,0:T(4,128)}, u32[]{:S(2)}) copy-start(f32[4,32,3,64]{3,2,1,0:T(4,128)} %fusion.53) | copy-start | bytes 294916
  248.5 8.4 %copy-start.19 = (f32[4,32,3,64]{3,2,1,0:T(4,128)S(1)}, f32[4,32,3,64]{3,2,1,0:T(4,128)}, u32[]{:S(2)}) copy-start(f32[4,32,3,64]{3,2,1,0:T(4,128)} %fusion.71) | copy-start | bytes 294916
  300.7 71.3 %copy-start.16 = (f32[4,2,4,32]{3,2,1,0:T(4,128)}, f32[4,2,4,32]{3,2,1,0:T(4,128)S(1)}, u32[]{:S(2)}) copy-start(f32[4,2,4,32]{3,2,1,0:T(4,128)S(1)} %pad_maximum_fusion) | copy-start | bytes 12292
where the time goes:
time: 380 us; the launch traced here: 375 us
  blocking collectives  135 us (36%)
  matrix products  117 us (31%)
  local copies, waits for them, and re-layouts  60.1 us (16%)
  other arithmetic  51 us (13%)
  starting transfers between devices  9.66 us (3%)
    all_gather x1, blocking collectives, per_device(): lax.all_gather(flow_field[None], ('gx', 'gy', 'sa'), axis=0, tiled=True)  69.3 us
    all_gather x1, blocking collectives, per_device(): lax.all_gather(weight[None], ('gx', 'gy', 'sa'), axis=0, tiled=True)  66.2 us
    dot_general x16, matrix products, transform_rows(): jnp.einsum('kx,axc->akc', row_table, blocks, preferred_element_type=jnp.f...  31.8 us
    convert_element_type x1, other arithmetic, refine(): prod_real = (cross_real / scale).astype(jnp.bfloat16)  27.3 us
    dot_general x4, matrix products, refine(): jnp.einsum('akbd,abke->abed', half_real, row_cos, preferred_element_type=...  24.8 us
    dot_general x4, matrix products, refine(): jnp.einsum('akbd,abke->abed', half_imag, row_sin, preferred_element_type=...  24.2 us
    convert_element_type x4, local copies, waits for them, and re-layouts, refine(): now_real = current[0].astype(jnp.float32).reshape(layout)  17.6 us
    convert_element_type x4, local copies, waits for them, and re-layouts, refine(): now_imag = current[1].astype(jnp.float32).reshape(layout)  14.1 us
  transfers between devices with their start and end apart: 2, of which 0 were waited for; matrix products, arithmetic and copies ran while one was open for 22% of the time, Pallas kernels for 0%

commit v1 on v0

v1 whole, which is shorter than its diff:
```python
import functools
import math

import jax
import jax.numpy as jnp
import ml_dtypes
import numpy as np
from jax import lax
from jax.experimental import pallas as pl
from jax.experimental.pallas import tpu as pltpu
from jax.sharding import PartitionSpec as P

PATCH = 64
HALF = PATCH // 2
RELAX = 8
GROUP = 8
CHUNK = GROUP * PATCH
SIDE = GROUP * HALF

spring_plane = 0.5
spring_stack = 1.0
step_size = 0.2
damping = 0.6
whiten_floor = 1024.0

MESH = pl.DeviceIdType.MESH
f32 = jnp.float32
bf16 = jnp.bfloat16


def cosine(m):
    angle = (np.asarray(m) % PATCH).astype(np.float32) * np.float32(2.0 * math.pi / PATCH)
    return np.cos(angle).astype(np.float32).astype(ml_dtypes.bfloat16).astype(np.float32)


def sine(m):
    angle = (np.asarray(m) % PATCH).astype(np.float32) * np.float32(2.0 * math.pi / PATCH)
    return np.sin(angle).astype(np.float32).astype(ml_dtypes.bfloat16).astype(np.float32)


@functools.lru_cache(maxsize=None)
def tables(patch_rows, patch_cols):
    y = np.arange(PATCH)
    k2 = np.arange(1, HALF + 1)
    col = np.zeros((4, PATCH, 2, 4, HALF), np.float32)
    for j in range(4):
        col[j, :, 0, j] = cosine(y[:, None] * k2)
        col[j, :, 1, j] = -sine(y[:, None] * k2)
    col = col.reshape(4 * PATCH, 8 * HALF)
    lanes = np.arange(patch_rows * patch_cols)
    zero = (np.arange(patch_cols * PATCH)[:, None] // PATCH == lanes % patch_cols).astype(np.float32)
    c = cosine(y[:, None] * y)
    s = sine(y[:, None] * y)
    row = np.block([[c, s], [-s, c]])
    row0 = np.concatenate([c, -s], 0)
    shift = np.arange(-3, 4)
    first = np.zeros((16, 2 * PATCH), np.float32)
    first[:7] = np.concatenate([cosine(shift[:, None] * y), -sine(shift[:, None] * y)], 1)
    first[8:15] = np.concatenate([sine(shift[:, None] * y), cosine(shift[:, None] * y)], 1)
    weight = np.where(k2 == HALF, 1.0, 2.0) / PATCH
    second = np.zeros((patch_cols // GROUP, 2, GROUP, HALF, 8, patch_cols), np.float32)
    for patch in range(patch_cols):
        at, j = divmod(patch, GROUP)
        second[at, 0, j, :, :7, patch] = weight[:, None] * cosine(k2[:, None] * shift)
        second[at, 1, j, :, :7, patch] = -weight[:, None] * sine(k2[:, None] * shift)
    second = second.reshape(patch_cols * PATCH, 8 * patch_cols)
    direct = np.zeros((lanes.size, 8, patch_cols), np.float32)
    direct[lanes, :7, lanes % patch_cols] = 1.0 / PATCH
    second = np.concatenate([second, direct.reshape(lanes.size, -1)], 0)
    return [t.astype(ml_dtypes.bfloat16) for t in (col, zero, row, row0, first, second)]


def dot(a, b):
    return jnp.dot(a, b, preferred_element_type=f32)


def whitened(now, old):
    now, old = now.astype(f32), old.astype(f32)
    now_real, now_imag = now[:PATCH], now[PATCH:]
    old_real, old_imag = old[:PATCH], old[PATCH:]
    cross_real = now_real * old_real + now_imag * old_imag
    cross_imag = now_imag * old_real - now_real * old_imag
    inverse = lax.rsqrt(
        cross_real * cross_real + cross_imag * cross_imag + whiten_floor * whiten_floor
    )
    return jnp.concatenate([cross_real * inverse, cross_imag * inverse], 0).astype(bf16)


def section_step(load, tabs, spec, spec0, sums, base, compare):
    col, zero, row, row0, first = [t[...] for t in tabs]
    patch_rows, unused, width = spec.shape
    chunks = width // SIDE
    lanes = spec0.shape[1]
    patch_cols = lanes // patch_rows
    totals = None
    for at in range(chunks):
        x = load(at)
        part = dot(x, zero[at * CHUNK:(at + 1) * CHUNK])
        totals = part if totals is None else totals + part
        halves = [
            dot(x[:, h * CHUNK // 2:(h + 1) * CHUNK // 2], col).astype(bf16) for h in range(2)
        ]
        real = jnp.concatenate([h[:, :SIDE // 2] for h in halves], 1)
        imag = jnp.concatenate([h[:, SIDE // 2:] for h in halves], 1)
        for a in range(patch_rows):
            part = slice(a * PATCH, (a + 1) * PATCH)
            now = dot(row, jnp.concatenate([real[part], imag[part]], 0)).astype(bf16)
            here = slice(at * SIDE, (at + 1) * SIDE)
            if compare:
                prod = whitened(now, spec[a, :, here])
                half = dot(first, prod)
                rows = pl.ds(base + a * 8, 8)
                sums[rows, at * CHUNK:at * CHUNK + SIDE] = half[:8]
                sums[rows, at * CHUNK + SIDE:(at + 1) * CHUNK] = half[8:]
            spec[a, :, here] = now
    lane = lax.broadcasted_iota(jnp.int32, (PATCH, lanes), 1) // patch_cols
    packed = jnp.zeros((PATCH, lanes), f32)
    for a in range(patch_rows):
        packed = jnp.where(lane == a, totals[a * PATCH:(a + 1) * PATCH], packed)
    now = dot(row0, packed.astype(bf16)).astype(bf16)
    if compare:
        half = dot(first, whitened(now, spec0[...]))[:8]
        for a in range(patch_rows):
            sums[pl.ds(base + a * 8, 8), chunks * CHUNK:] = jnp.where(lane[:8] == a, half, 0.0)
    spec0[...] = now


def pick(sums, second, peaks, patch_cols):
    corr = dot(sums.astype(bf16), second)
    count = corr.shape[0] // 8
    width = corr.shape[1]
    corr = corr.reshape(count, 8, width)
    p1, p2 = peaks[0], peaks[1]
    sub = lax.broadcasted_iota(jnp.int32, (count, 8, width), 1).astype(f32) - 3.0
    shift = lax.broadcasted_iota(jnp.int32, (count, width), 1) // patch_cols
    shift = shift.astype(f32) - 3.0
    p1_all = jnp.broadcast_to(p1[:, None, :], (count, 8, width))
    at1 = [jnp.sum(jnp.where(sub == p1_all + d, corr, 0.0), 1) for d in (-1.0, 0.0, 1.0)]

    def fold(values, d):
        values = jnp.where(shift == p2 + d, values, 0.0)
        reach = width // 2
        while reach >= patch_cols:
            values = values + pltpu.roll(values, reach, 1)
            reach //= 2
        return values

    center = fold(at1[1], 0.0)

    def step(low, high):
        return (low - high) / (2.0 * jnp.maximum(jnp.abs(low - 2.0 * center + high), 1.0))

    row_flow = p1 + step(fold(at1[0], 0.0), fold(at1[2], 0.0))
    col_flow = p2 + step(fold(at1[1], -1.0), fold(at1[1], 1.0))
    return row_flow, col_flow


def inner_kernel(count, pix, peaks, *refs):
    tabs, second, flow, spec, spec0, sums = refs[:5], refs[5], refs[6], refs[7], refs[8], refs[9]
    section = pl.program_id(0)
    patch_rows = spec.shape[0]
    patch_cols = spec0.shape[1] // patch_rows
    load = lambda at: pix[0, :, at * CHUNK:(at + 1) * CHUNK]

    @pl.when(section == 0)
    def _():
        section_step(load, tabs, spec, spec0, sums, 0, False)

    @pl.when(section > 0)
    def _():
        base = pl.multiple_of((section - 1) * patch_rows * 8, 8)
        section_step(load, tabs, spec, spec0, sums, base, True)

    @pl.when(section == count - 1)
    def _():
        flow[0], flow[1] = pick(sums[...], second[...], peaks, patch_cols)


def edge_kernel(top_old, low_old, top_now, low_now, peaks, *refs):
    tabs, second, flow, spec, spec0, sums = refs[:5], refs[5], refs[6], refs[7], refs[8], refs[9]
    patch_rows = spec.shape[0]
    patch_cols = spec0.shape[1] // patch_rows

    def pair(top, low):
        def load(at):
            here = slice(at * CHUNK, (at + 1) * CHUNK)
            return jnp.concatenate([top[0, :, here], low[0, :, here]], 0)
        return load

    section_step(pair(top_old, low_old), tabs, spec, spec0, sums, 0, False)
    section_step(pair(top_now, low_now), tabs, spec, spec0, sums, 0, True)
    flow[0], flow[1] = pick(sums[...], second[...], peaks, patch_cols)


def scratch(patch_rows, patch_cols, entries):
    return [
        pltpu.VMEM((patch_rows, 2 * PATCH, patch_cols * HALF), bf16),
        pltpu.VMEM((2 * PATCH, patch_rows * patch_cols), bf16),
        pltpu.VMEM((entries * 8, patch_cols * PATCH + patch_rows * patch_cols), f32),
    ]


def whole(array):
    return pl.BlockSpec(array.shape, lambda i: (0,) * array.ndim)


def inner_flow(pixels, peaks, tabs, patch_rows, patch_cols):
    count, height, width = pixels.shape
    entries = peaks.shape[1]
    return pl.pallas_call(
        functools.partial(inner_kernel, count),
        grid=(count,),
        in_specs=[pl.BlockSpec((1, height, width), lambda i: (i, 0, 0)), whole(peaks)]
        + [whole(t) for t in tabs],
        out_specs=pl.BlockSpec(peaks.shape, lambda i: (0, 0, 0)),
        out_shape=jax.ShapeDtypeStruct(peaks.shape, f32),
        scratch_shapes=scratch(patch_rows, patch_cols, entries),
        compiler_params=pltpu.CompilerParams(
            dimension_semantics=("arbitrary",), vmem_limit_bytes=32 * 1024 * 1024
        ),
        cost_estimate=pl.CostEstimate(
            flops=count * height * width * 2048, bytes_accessed=2 * pixels.size, transcendentals=0
        ),
        name="inner_flow",
    )(pixels, peaks, *tabs)


def edge_flow(pixels, from_last, from_next, peaks, tabs, patch_rows, patch_cols):
    count, height, width = pixels.shape
    block = (1, height // 2, width)
    return pl.pallas_call(
        edge_kernel,
        grid=(1,),
        in_specs=[
            pl.BlockSpec(block, lambda i: (0, 0, 0)),
            pl.BlockSpec(block, lambda i: (count - 1, 1, 0)),
            pl.BlockSpec(block, lambda i: (0, 0, 0)),
            pl.BlockSpec(block, lambda i: (0, 0, 0)),
            whole(peaks),
        ]
        + [whole(t) for t in tabs],
        out_specs=pl.BlockSpec(peaks.shape, lambda i: (0, 0, 0)),
        out_shape=jax.ShapeDtypeStruct(peaks.shape, f32),
        scratch_shapes=scratch(patch_rows, patch_cols, patch_rows),
        compiler_params=pltpu.CompilerParams(
            dimension_semantics=("arbitrary",), vmem_limit_bytes=32 * 1024 * 1024
        ),
        cost_estimate=pl.CostEstimate(
            flops=height * width * 4096, bytes_accessed=4 * height * width, transcendentals=0
        ),
        name="edge_flow",
    )(from_last, pixels, pixels, from_next, peaks, *tabs)


def gather_kernel(sizes, own, out, send, recv):
    size_x, size_y, size_s = sizes
    total = size_x * size_y * size_s
    me = (lax.axis_index("gx") * size_y + lax.axis_index("gy")) * size_s + lax.axis_index("sa")

    def place(i):
        there = lax.rem(me + i, total)
        return there // (size_y * size_s), lax.rem(there // size_s, size_y), lax.rem(there, size_s)

    barrier = pltpu.get_barrier_semaphore()

    @pl.loop(1, total)
    def _(i):
        pl.semaphore_signal(barrier, inc=1, device_id=place(i), device_id_type=MESH)

    pl.semaphore_wait(barrier, total - 1)

    def copy(i):
        return pltpu.make_async_remote_copy(
            src_ref=own,
            dst_ref=out.at[total - i],
            send_sem=send.at[i],
            recv_sem=recv.at[total - i],
            device_id=place(i),
            device_id_type=MESH,
        )

    @pl.loop(1, total)
    def _(i):
        copy(i).start()

    out[0] = own[...]

    @pl.loop(1, total)
    def _(i):
        copy(i).wait()


def gather(payload, sizes):
    total = math.prod(sizes)
    got = pl.pallas_call(
        functools.partial(gather_kernel, sizes),
        out_shape=jax.ShapeDtypeStruct((total,) + payload.shape, payload.dtype),
        in_specs=[pl.BlockSpec(memory_space=pltpu.VMEM)],
        out_specs=pl.BlockSpec(memory_space=pltpu.VMEM),
        scratch_shapes=[
            pltpu.SemaphoreType.DMA((total,)),
            pltpu.SemaphoreType.DMA((total,)),
        ],
        compiler_params=pltpu.CompilerParams(collective_id=0, has_side_effects=True),
        name="gather_flow",
    )(payload)
    me = (lax.axis_index("gx") * sizes[1] + lax.axis_index("gy")) * sizes[2] + lax.axis_index("sa")
    return jnp.roll(got, me, axis=0)


def edge_degree(row_index, col_index, total_rows, total_cols):
    return (
        4.0
        - (row_index == 0).astype(f32)
        - (row_index == total_rows - 1).astype(f32)
        - (col_index == 0).astype(f32)
        - (col_index == total_cols - 1).astype(f32)
    )


def relax_kernel(flow, weight, out, state):
    sections, parts, total_rows, total_cols = flow.shape
    w = weight[...][:, None]
    f = flow[...]
    running = f[0]
    state[0] = running
    for s in range(1, sections):
        running = running + f[s]
        state[s] = running
    row = lax.broadcasted_iota(jnp.int32, (total_rows, total_cols), 0)
    col = lax.broadcasted_iota(jnp.int32, (total_rows, total_cols), 1)
    degree = edge_degree(row, col, total_rows, total_cols)
    shape = (sections, parts, total_rows, total_cols)
    row4 = jnp.broadcast_to(row, shape)
    col4 = jnp.broadcast_to(col, shape)
    nothing = jnp.zeros((1,) + shape[1:], f32)
    w_next = jnp.concatenate([w[1:], jnp.zeros_like(w[:1])], 0)
    f_next = jnp.concatenate([f[1:], nothing], 0)

    def step(unused, carry):
        now, velocity = carry
        around = (
            jnp.where(row4 == 0, 0.0, pltpu.roll(now, 1, 2))
            + jnp.where(row4 == total_rows - 1, 0.0, pltpu.roll(now, total_rows - 1, 2))
            + jnp.where(col4 == 0, 0.0, pltpu.roll(now, 1, 3))
            + jnp.where(col4 == total_cols - 1, 0.0, pltpu.roll(now, total_cols - 1, 3))
        )
        lower = jnp.concatenate([nothing, now[:-1]], 0)
        upper = jnp.concatenate([now[1:], nothing], 0)
        here_term = w * (now - lower - f)
        next_term = w_next * (upper - now - f_next)
        gradient = spring_plane * (degree * now - around) + spring_stack * (here_term - next_term)
        velocity = damping * velocity - step_size * gradient
        return now + velocity, velocity

    final, unused_velocity = lax.fori_loop(
        0, RELAX, step, (state[...], jnp.zeros(shape, f32))
    )
    out[...] = final


def relax(flow, weight):
    return pl.pallas_call(
        relax_kernel,
        out_shape=jax.ShapeDtypeStruct(flow.shape, f32),
        in_specs=[pl.BlockSpec(memory_space=pltpu.VMEM)] * 2,
        out_specs=pl.BlockSpec(memory_space=pltpu.VMEM),
        scratch_shapes=[pltpu.VMEM(flow.shape, f32)],
        compiler_params=pltpu.CompilerParams(vmem_limit_bytes=32 * 1024 * 1024),
        name="relax",
    )(flow, weight)


def per_device(pixels, peak_offsets, validity):
    count, height, width = pixels.shape
    patch_rows, patch_cols = peak_offsets.shape[2:]
    half_rows = patch_rows // 2
    sizes = tuple(lax.axis_size(axis) for axis in ("gx", "gy", "sa"))
    size_x, size_y, size_s = sizes
    ahead = [(i, i + 1) for i in range(size_s - 1)]
    back = [(i + 1, i) for i in range(size_s - 1)]
    ring = [(i, (i - 1) % size_s) for i in range(size_s)]
    from_last = lax.ppermute(pixels[count - 1:, :height // 2], "sa", ahead)
    from_next = lax.ppermute(pixels[:1, height // 2:], "sa", back)
    peaks = peak_offsets.astype(f32)
    next_peaks = lax.ppermute(peaks[0, :, half_rows:], "sa", ring)
    edge_peaks = jnp.concatenate([peaks[0, :, :half_rows], next_peaks], 1)
    inner_peaks = jnp.transpose(peaks[1:], (1, 0, 2, 3)).reshape(2, -1, patch_cols)
    tabs = [jnp.asarray(t) for t in tables(patch_rows, patch_cols)]
    inner = inner_flow(pixels, jnp.tile(inner_peaks, (1, 1, 8)), tabs, patch_rows, patch_cols)
    edge = edge_flow(
        pixels, from_last, from_next, jnp.tile(edge_peaks, (1, 1, 8)), tabs, patch_rows, patch_cols
    )
    inner = inner[:, :, :patch_cols].reshape(2, count - 1, patch_rows * patch_cols)
    edge = edge[:, :, :patch_cols].reshape(2, 1, patch_rows * patch_cols)
    flows = jnp.concatenate([edge, inner], 1)
    weight = validity.astype(f32).reshape(1, count, patch_rows * patch_cols)
    payload = jnp.concatenate([flows, weight], 0).reshape(3 * count, patch_rows * patch_cols)
    everyone = gather(payload, sizes)
    blocks = everyone.reshape(size_x, size_y, size_s, 3, count, patch_rows, patch_cols)
    low = jnp.roll(blocks[:, :, :, :2, :1, half_rows:], 1, axis=2)
    low = jnp.concatenate([low, blocks[:, :, :, 2:, :1, half_rows:]], 3)
    begin = jnp.concatenate([blocks[:, :, :, :, :1, :half_rows], low], 5)
    blocks = jnp.concatenate([begin, blocks[:, :, :, :, 1:]], 4)
    blocks = jnp.transpose(blocks, (2, 4, 3, 1, 5, 0, 6))
    blocks = blocks.reshape(size_s * count, 3, size_y * patch_rows, size_x * patch_cols)
    all_flow, all_weight = blocks[:, :2], blocks[:, 2]
    final = relax(all_flow, all_weight)
    zero = jnp.zeros((), jnp.int32)
    starts = (
        lax.axis_index("sa") * count,
        zero,
        lax.axis_index("gy") * patch_rows,
        lax.axis_index("gx") * patch_cols,
    )
    shape = (count, 2, patch_rows, patch_cols)
    return lax.dynamic_slice(all_flow, starts, shape), lax.dynamic_slice(final, starts, shape)


def solution(mesh):
    return jax.shard_map(
        per_device,
        mesh=mesh,
        in_specs=(P("sa", "gy", "gx"), P("sa", None, "gy", "gx"), P("sa", "gy", "gx")),
        out_specs=(P("sa", None, "gy", "gx"), P("sa", None, "gy", "gx")),
        check_vma=False,
    )
```

time: 380 us -> 64.6 us (0.17); the launches traced: 375 us -> 64 us
  blocking collectives: 135 us -> 0 us
  matrix products: 117 us -> 0 us
  other arithmetic: 51 us -> 2.11 us
  local copies, waits for them, and re-layouts: 60.1 us -> 15.8 us
  Pallas kernels: 0 us -> 34.2 us
    all_gather x2 -> x0, blocking collectives: 135 us -> none  [the longest x1 69.3 us: per_device(): lax.all_gather(flow_field[None], ('gx', 'gy', 'sa'), axis=0, tiled=True)]
    dot_general x40 -> x0, matrix products: 117 us -> none  [the longest x16 31.8 us: transform_rows(): jnp.einsum('kx,axc->akc', row_table, blocks, preferred_element_type=jnp.f...]
    convert_element_type x7 -> x2, other arithmetic: 38.4 us -> 0.73 us  [the longest x1 0.72 us: per_device(): peaks = peak_offsets.astype(f32)]
    convert_element_type x16 -> x0, local copies, waits for them, and re-layouts: 37.5 us -> none  [the longest x4 17.6 us: refine(): now_real = current[0].astype(jnp.float32).reshape(layout)]
    pallas_call x0 -> x4, Pallas kernels: none -> 34.2 us  [the longest x1 15.1 us: inner_flow(): pl.pallas_call(functools.partial(inner_kernel, count), grid=(count,), in_...]
    reshape x12 -> x6, local copies, waits for them, and re-layouts: 15.1 us -> 1.57 us  [the longest x1 0.61 us: per_device(): jnp.concatenate([flows, weight], 0)]
    unnamed x44 -> x31, local copies, waits for them, and re-layouts: 0.1 us -> 10.4 us
    slice x4 -> x0, other arithmetic: 9.04 us -> none  [subpixel(): row_low = correlation[..., 0, 1]]
  transfers between devices with their start and end apart: 2 -> 3, of which waited for: 0 -> 0; matrix products, arithmetic and copies ran while one was open for 22% -> 4% of each run, Pallas kernels for 0% -> 24%
where the time goes in v1:
time: 64.6 us; the launch traced here: 64 us
  Pallas kernels  34.2 us (53%)
  local copies, waits for them, and re-layouts  15.8 us (24%)
  starting transfers between devices  10.9 us (17%)
  other arithmetic  2.11 us (3%)
  between operations  0.99 us (2%)
    pallas_call x1, Pallas kernels, inner_flow(): pl.pallas_call(functools.partial(inner_kernel, count), grid=(count,), in_...  15.1 us
    pallas_call x1, Pallas kernels, gather(): pl.pallas_call(functools.partial(gather_kernel, sizes), out_shape=jax.Sha...  11.9 us
    unnamed x31, local copies, waits for them, and re-layouts  10.4 us
    pallas_call x1, Pallas kernels, edge_flow(): pl.pallas_call(edge_kernel, grid=(1,), in_specs=[pl.BlockSpec(block, lamb...  5.9 us
    ppermute x1, starting transfers between devices, per_device(): next_peaks = lax.ppermute(peaks[0, :, half_rows:], 'sa', ring)  5.05 us
    ppermute x1, starting transfers between devices, per_device(): from_last = lax.ppermute(pixels[count - 1:, :height // 2], 'sa', ahead)  4.58 us
    slice x1, local copies, waits for them, and re-layouts, per_device(): from_next = lax.ppermute(pixels[:1, height // 2:], 'sa', back)  2.09 us
  transfers between devices with their start and end apart: 3, of which 0 were waited for; matrix products, arithmetic and copies ran while one was open for 4% of the time, Pallas kernels for 24%

profile of v1, /device:TPU:0, one launch (start us, length us, event | category | flops | bytes accessed | tf_op | source)
XLA Modules:
  0.0 64.0 jit_solution(8412493649963773284)
XLA Ops:
  0.6 0.7 %convert_element_type.6 = f32[4,2,4,32]{3,2,1,0:T(4,128)S(1)} convert(s32[4,2,4,32]{3,2,1,0:T(4,128)} %param.10) | non-fusion elementwise | flops 1024 | bytes 8192 | tf_op jit(solution)/shard_map/convert_element_type | solution.py:385
  1.4 5.0 %collective-permute-start.2 = (f32[2,2,32]{2,1,0:T(2,128)S(1)}, f32[2,2,32]{2,1,0:T(2,128)S(1)}, u32[]{:S(2)}, u32[]{:S(2)}) collective-permute-start(f32[2,2,32]{2,1,0:T(2,128)S(1)} %get-tuple-element.9), channel_id=1, source_target_pairs={{0,3},{1,0},{2,1},{3,2},{4,7},{5,4},{6,5},{7,6},{8,11},{9,8},{10,9... | collective-permute-start | bytes 1544 | tf_op jit(solution)/shard_map/ppermute | solution.py:386
  6.4 2.1 %fusion.1 = (bf16[1,128,2048]{2,1,0:T(8,128)(2,1)}, bf16[1,128,2048]{2,1,0:T(8,128)(2,1)S(1)}) fusion(bf16[4,256,2048]{2,1,0:T(8,128)(2,1)} %pix.1), kind=kLoop, calls=%fused_computation.12 | loop fusion | bytes 2097152 | tf_op jit(solution)/shard_map/slice | solution.py:384
  8.5 1.3 %collective-permute-start.1 = (bf16[1,128,2048]{2,1,0:T(8,128)(2,1)}, bf16[1,128,2048]{2,1,0:T(8,128)(2,1)S(1)}, u32[]{:S(2)}, u32[]{:S(2)}) collective-permute-start(bf16[1,128,2048]{2,1,0:T(8,128)(2,1)} %get-tuple-element.6), channel_id=1, source_target_pairs={{1,0},{2,1},{3,2},{5,4},{6,5},{7,6},{9,8},{10,9},{11,10},{13,12},{... | collective-permute-start | bytes 1572872 | tf_op jit(solution)/shard_map/ppermute | solution.py:384
  9.8 4.6 %collective-permute-start = (bf16[1,128,2048]{2,1,0:T(8,128)(2,1)S(1)}, bf16[1,128,2048]{2,1,0:T(8,128)(2,1)S(1)}, u32[]{:S(2)}, u32[]{:S(2)}) collective-permute-start(bf16[1,128,2048]{2,1,0:T(8,128)(2,1)S(1)} %get-tuple-element.7), channel_id=1, source_target_pairs={{0,1},{1,2},{2,3},{4,5},{5,6},{6,7},{8,9},{9,10},{10,11},{12,13},{... | collective-permute-start | bytes 1572872 | tf_op jit(solution)/shard_map/ppermute | solution.py:383
  14.4 0.1 tile.23
  14.5 0.0 copy-start
  14.6 2.2 %copy-done = bf16[4,256,2048]{2,1,0:T(8,128)(2,1)S(1)} copy-done((bf16[4,256,2048]{2,1,0:T(8,128)(2,1)S(1)}, bf16[4,256,2048]{2,1,0:T(8,128)(2,1)}, u32[]{:S(2)}) %copy-start) | copy-done | bytes 4194328
  16.7 0.0 copy-start.2
  16.7 1.2 %copy-done.2 = bf16[2176,256]{1,0:T(8,128)(2,1)S(1)} copy-done((bf16[2176,256]{1,0:T(8,128)(2,1)S(1)}, bf16[2176,256]{1,0:T(8,128)(2,1)}, u32[]{:S(2)}) %copy-start.2) | copy-done | bytes 1114136
  18.0 1.0 %copy-done.4 = bf16[2048,128]{1,0:T(8,128)(2,1)S(1)} copy-done((bf16[2048,128]{1,0:T(8,128)(2,1)S(1)}, bf16[2048,128]{1,0:T(8,128)(2,1)}, u32[]{:S(2)}) %copy-start.4) | copy-done | bytes 524312
  19.0 0.9 %copy-done.6 = bf16[256,256]{1,0:T(8,128)(2,1)S(1)} copy-done((bf16[256,256]{1,0:T(8,128)(2,1)S(1)}, bf16[256,256]{1,0:T(8,128)(2,1)}, u32[]{:S(2)}) %copy-start.6) | copy-done | bytes 131096
  19.9 0.8 %copy-done.8 = bf16[128,64]{1,0:T(8,128)(2,1)S(1)} copy-done((bf16[128,64]{1,0:T(8,128)(2,1)S(1)}, bf16[128,64]{1,0:T(8,128)(2,1)}, u32[]{:S(2)}) %copy-start.8) | copy-done | bytes 16408
  20.7 0.8 %copy-done.10 = bf16[128,128]{1,0:T(8,128)(2,1)S(1)} copy-done((bf16[128,128]{1,0:T(8,128)(2,1)S(1)}, bf16[128,128]{1,0:T(8,128)(2,1)}, u32[]{:S(2)}) %copy-start.10) | copy-done | bytes 32792
  21.5 0.7 %copy-done.12 = bf16[16,128]{1,0:T(8,128)(2,1)S(1)} copy-done((bf16[16,128]{1,0:T(8,128)(2,1)S(1)}, bf16[16,128]{1,0:T(8,128)(2,1)}, u32[]{:S(2)}) %copy-start.12) | copy-done | bytes 4120
  22.1 0.0 copy-start.9
  22.2 0.0 copy-start.11
  22.2 0.0 copy-start.13
  22.2 15.1 %inner_flow.1 = f32[2,12,256]{2,1,0:T(8,128)S(1)} custom-call(bf16[4,256,2048]{2,1,0:T(8,128)(2,1)S(1)} %copy-done, f32[2,12,256]{2,1,0:T(8,128)S(1)} %copy.15.peaks, bf16[256,256]{1,0:T(8,128)(2,1)S(1)} %copy-done.6, bf16[2048,128]{1,0:T(8,128)(2,1)S(1)} %copy-done.4, bf16[128,128]{1,0:T(8,128)(2,1)S(1)} %copy-done.10, bf16[128,64]{1,0:T(8,128)(2,1)S(1)} %copy-done.8, ...), custom_call_target="tpu_custom_call" | custom-call | flops 4294967296 | bytes 4194304 | tf_op jit(solution)/shard_map/inner_flow/pallas_call | solution.py:210
  37.3 0.0 copy-done.14
  37.3 0.1 reshape.32
  37.4 0.1 reshape.31
  37.5 0.0 collective-permute-done.2
  37.5 0.1 tile.20.peaks
  37.6 0.0 collective-permute-done.1.low_now
  37.6 0.0 collective-permute-done.top_old
  37.6 0.0 copy-done.3
  37.6 0.0 copy-done.5
  37.6 0.0 copy-done.7
  37.6 0.0 copy-done.9
  37.7 0.0 copy-done.11
  37.7 0.0 copy-done.13
  37.7 0.0 copy-start.1
  37.7 2.2 %copy-done.1 = bf16[4,256,2048]{2,1,0:T(8,128)(2,1)S(1)} copy-done((bf16[4,256,2048]{2,1,0:T(8,128)(2,1)S(1)}, bf16[4,256,2048]{2,1,0:T(8,128)(2,1)}, u32[]{:S(2)}) %copy-start.1) | copy-done | bytes 4194328
  39.9 5.9 %edge_flow.1 = f32[2,4,256]{2,1,0:T(4,128)S(1)} custom-call(bf16[1,128,2048]{2,1,0:T(8,128)(2,1)S(1)} %collective-permute-done.top_old, bf16[4,256,2048]{2,1,0:T(8,128)(2,1)S(1)} %copy-done.1, bf16[4,256,2048]{2,1,0:T(8,128)(2,1)S(1)} %copy-done.1, bf16[1,128,2048]{2,1,0:T(8,128)(2,1)S(1)} %collective-permute-done.1.low_now, f32[2,4,256]{2,1,0:T(4,128)S(1)} %tile.20.peaks, ...), custom_call_target="tpu_custom_call" | custom-call | flops 2147483648 | bytes 2097152 | tf_op jit(solution)/shard_map/edge_flow/pallas_call | solution.py:231
  45.8 0.1 reshape.30
  45.9 0.6 reshape.33.own
  46.5 11.9 %gather_flow.1 = f32[32,12,128]{2,1,0:T(8,128)} custom-call(f32[12,128]{1,0:T(8,128)} %reshape.33.own), custom_call_target="tpu_custom_call" | custom-call | tf_op jit(solution)/shard_map/gather_flow/pallas_call | solution.py:295
  58.4 1.0 %fusion = f32[32,12,128]{2,1,0:T(8,128)S(1)} fusion(s32[]{:T(128)S(6)} %select_n.26, f32[32,12,128]{2,1,0:T(8,128)} %gather_flow.1), kind=kLoop, calls=%fused_computation.3 | loop fusion | flops 49152 | bytes 393220 | tf_op jit(solution)/shard_map/jit(_roll_dynamic)/concatenate | solution.py:308
  59.4 0.1 copy.17
  59.5 0.3 reshape.34
  60.1 0.3 maximum_bitcast_fusion
  60.4 0.5 copy.18
  60.9 0.4 reshape.35
  61.3 1.3 %relax.1 = f32[16,2,8,128]{3,2,1,0:T(8,128)S(1)} custom-call(f32[16,2,8,128]{3,2,1,0:T(8,128)S(1)} %copy.19.flow, f32[16,8,128]{2,1,0:T(8,128)S(1)} %slice_bitcast_fusion.weight), custom_call_target="tpu_custom_call" | custom-call | tf_op jit(solution)/shard_map/relax/pallas_call | solution.py:363
  62.6 0.1 constant_dynamic-slice_fusion.1
  62.7 0.7 %constant_dynamic-slice_fusion = f32[4,2,4,32]{3,2,1,0:T(4,128)} fusion(f32[16,2,8,128]{3,2,1,0:T(8,128)S(1)} %relax.1, s32[]{:T(128)S(6)} %select_n.27, s32[]{:T(128)S(6)} %select_n.28, s32[]{:T(128)S(6)} %select_n.29), kind=kLoop, calls=%fused_computation.10 | loop fusion | bytes 8204 | tf_op jit(solution)/shard_map/dynamic_slice | solution.py:417
  63.4 0.6 copy.20
  (28 shorter events, 0.2 us)
Async XLA Ops:
  1.4 36.1 %collective-permute-start.2 = (f32[2,2,32]{2,1,0:T(2,128)S(1)}, f32[2,2,32]{2,1,0:T(2,128)S(1)}, u32[]{:S(2)}, u32[]{:S(2)}) collective-permute-start(f32[2,2,32]{2,1,0:T(2,128)S(1)} %get-tuple-element.9), channel_id=1, source_target_pairs={{0,3},{1,0},{2,1},{3,2},{4,7},{5,4},{6,5},{7,6},{8,11},{9,8},{10,9... | collective-permute-start | bytes 1544 | tf_op jit(solution)/shard_map/ppermute | solution.py:386
  8.5 29.1 %collective-permute-start.1 = (bf16[1,128,2048]{2,1,0:T(8,128)(2,1)}, bf16[1,128,2048]{2,1,0:T(8,128)(2,1)S(1)}, u32[]{:S(2)}, u32[]{:S(2)}) collective-permute-start(bf16[1,128,2048]{2,1,0:T(8,128)(2,1)} %get-tuple-element.6), channel_id=1, source_target_pairs={{1,0},{2,1},{3,2},{5,4},{6,5},{7,6},{9,8},{10,9},{11,10},{13,12},{... | collective-permute-start | bytes 1572872 | tf_op jit(solution)/shard_map/ppermute | solution.py:384
  9.8 27.8 %collective-permute-start = (bf16[1,128,2048]{2,1,0:T(8,128)(2,1)S(1)}, bf16[1,128,2048]{2,1,0:T(8,128)(2,1)S(1)}, u32[]{:S(2)}, u32[]{:S(2)}) collective-permute-start(bf16[1,128,2048]{2,1,0:T(8,128)(2,1)S(1)} %get-tuple-element.7), channel_id=1, source_target_pairs={{0,1},{1,2},{2,3},{4,5},{5,6},{6,7},{8,9},{9,10},{10,11},{12,13},{... | collective-permute-start | bytes 1572872 | tf_op jit(solution)/shard_map/ppermute | solution.py:383
  14.5 2.2 %copy-start = (bf16[4,256,2048]{2,1,0:T(8,128)(2,1)S(1)}, bf16[4,256,2048]{2,1,0:T(8,128)(2,1)}, u32[]{:S(2)}) copy-start(bf16[4,256,2048]{2,1,0:T(8,128)(2,1)} %pix.1) | copy-start | bytes 12582916
  16.7 1.2 %copy-start.2 = (bf16[2176,256]{1,0:T(8,128)(2,1)S(1)}, bf16[2176,256]{1,0:T(8,128)(2,1)}, u32[]{:S(2)}) copy-start(bf16[2176,256]{1,0:T(8,128)(2,1)} %constant.63.clone.refs_5_) | copy-start | bytes 3342340
  18.0 1.0 %copy-start.4 = (bf16[2048,128]{1,0:T(8,128)(2,1)S(1)}, bf16[2048,128]{1,0:T(8,128)(2,1)}, u32[]{:S(2)}) copy-start(bf16[2048,128]{1,0:T(8,128)(2,1)} %constant.59.clone.refs_1_) | copy-start | bytes 1572868
  19.0 0.9 %copy-start.6 = (bf16[256,256]{1,0:T(8,128)(2,1)S(1)}, bf16[256,256]{1,0:T(8,128)(2,1)}, u32[]{:S(2)}) copy-start(bf16[256,256]{1,0:T(8,128)(2,1)} %constant.58.clone.refs_0_) | copy-start | bytes 393220
  19.9 0.8 %copy-start.8 = (bf16[128,64]{1,0:T(8,128)(2,1)S(1)}, bf16[128,64]{1,0:T(8,128)(2,1)}, u32[]{:S(2)}) copy-start(bf16[128,64]{1,0:T(8,128)(2,1)} %constant.61.clone.refs_3_) | copy-start | bytes 49156
  20.7 0.8 %copy-start.10 = (bf16[128,128]{1,0:T(8,128)(2,1)S(1)}, bf16[128,128]{1,0:T(8,128)(2,1)}, u32[]{:S(2)}) copy-start(bf16[128,128]{1,0:T(8,128)(2,1)} %constant.60.clone.refs_2_) | copy-start | bytes 98308
  21.5 0.7 %copy-start.12 = (bf16[16,128]{1,0:T(8,128)(2,1)S(1)}, bf16[16,128]{1,0:T(8,128)(2,1)}, u32[]{:S(2)}) copy-start(bf16[16,128]{1,0:T(8,128)(2,1)} %constant.62.clone.refs_4_) | copy-start | bytes 12292
  22.1 15.2 %copy-start.14 = (s32[4,4,32]{2,1,0:T(4,128)S(1)}, s32[4,4,32]{2,1,0:T(4,128)}, u32[]{:S(2)}) copy-start(s32[4,4,32]{2,1,0:T(4,128)} %param.11) | copy-start | bytes 6148
  22.1 15.5 %copy-start.3 = (bf16[2176,256]{1,0:T(8,128)(2,1)S(1)}, bf16[2176,256]{1,0:T(8,128)(2,1)}, u32[]{:S(2)}) copy-start(bf16[2176,256]{1,0:T(8,128)(2,1)} %constant.63.clone.refs_5_) | copy-start | bytes 3342340
  22.1 15.5 %copy-start.5 = (bf16[2048,128]{1,0:T(8,128)(2,1)S(1)}, bf16[2048,128]{1,0:T(8,128)(2,1)}, u32[]{:S(2)}) copy-start(bf16[2048,128]{1,0:T(8,128)(2,1)} %constant.59.clone.refs_1_) | copy-start | bytes 1572868
  22.1 15.5 %copy-start.7 = (bf16[256,256]{1,0:T(8,128)(2,1)S(1)}, bf16[256,256]{1,0:T(8,128)(2,1)}, u32[]{:S(2)}) copy-start(bf16[256,256]{1,0:T(8,128)(2,1)} %constant.58.clone.refs_0_) | copy-start | bytes 393220
  22.1 15.5 %copy-start.9 = (bf16[128,64]{1,0:T(8,128)(2,1)S(1)}, bf16[128,64]{1,0:T(8,128)(2,1)}, u32[]{:S(2)}) copy-start(bf16[128,64]{1,0:T(8,128)(2,1)} %constant.61.clone.refs_3_) | copy-start | bytes 49156
  22.2 15.5 %copy-start.11 = (bf16[128,128]{1,0:T(8,128)(2,1)S(1)}, bf16[128,128]{1,0:T(8,128)(2,1)}, u32[]{:S(2)}) copy-start(bf16[128,128]{1,0:T(8,128)(2,1)} %constant.60.clone.refs_2_) | copy-start | bytes 98308
  22.2 15.5 %copy-start.13 = (bf16[16,128]{1,0:T(8,128)(2,1)S(1)}, bf16[16,128]{1,0:T(8,128)(2,1)}, u32[]{:S(2)}) copy-start(bf16[16,128]{1,0:T(8,128)(2,1)} %constant.62.clone.refs_4_) | copy-start | bytes 12292
  37.7 2.2 %copy-start.1 = (bf16[4,256,2048]{2,1,0:T(8,128)(2,1)S(1)}, bf16[4,256,2048]{2,1,0:T(8,128)(2,1)}, u32[]{:S(2)}) copy-start(bf16[4,256,2048]{2,1,0:T(8,128)(2,1)} %pix.1) | copy-start | bytes 12582916

commit v2 on v1

v2 whole, which is shorter than its diff:
```python
import functools
import math

import jax
import jax.numpy as jnp
import ml_dtypes
import numpy as np
from jax import lax
from jax.experimental import pallas as pl
from jax.experimental.pallas import tpu as pltpu
from jax.sharding import PartitionSpec as P

PATCH = 64
HALF = PATCH // 2
RELAX = 8
GROUP = 8
CHUNK = GROUP * PATCH
SIDE = GROUP * HALF

spring_plane = 0.5
spring_stack = 1.0
step_size = 0.2
damping = 0.6
whiten_floor = 1024.0

MESH = pl.DeviceIdType.MESH
f32 = jnp.float32
bf16 = jnp.bfloat16


def cosine(m):
    angle = (np.asarray(m) % PATCH).astype(np.float32) * np.float32(2.0 * math.pi / PATCH)
    return np.cos(angle).astype(np.float32).astype(ml_dtypes.bfloat16).astype(np.float32)


def sine(m):
    angle = (np.asarray(m) % PATCH).astype(np.float32) * np.float32(2.0 * math.pi / PATCH)
    return np.sin(angle).astype(np.float32).astype(ml_dtypes.bfloat16).astype(np.float32)


@functools.lru_cache(maxsize=None)
def tables(patch_rows, patch_cols):
    y = np.arange(PATCH)
    k2 = np.arange(1, HALF + 1)
    col = np.zeros((4, PATCH, 2, 4, HALF), np.float32)
    for j in range(4):
        col[j, :, 0, j] = cosine(y[:, None] * k2)
        col[j, :, 1, j] = -sine(y[:, None] * k2)
    col = col.reshape(4 * PATCH, 8 * HALF)
    lanes = np.arange(patch_rows * patch_cols)
    zero = (np.arange(patch_cols * PATCH)[:, None] // PATCH == lanes % patch_cols).astype(np.float32)
    c = cosine(y[:, None] * y)
    s = sine(y[:, None] * y)
    row = np.block([[c, s], [-s, c]])
    row0 = np.concatenate([c, -s], 0)
    shift = np.arange(-3, 4)
    first = np.zeros((16, 2 * PATCH), np.float32)
    first[:7] = np.concatenate([cosine(shift[:, None] * y), -sine(shift[:, None] * y)], 1)
    first[8:15] = np.concatenate([sine(shift[:, None] * y), cosine(shift[:, None] * y)], 1)
    weight = np.where(k2 == HALF, 1.0, 2.0) / PATCH
    second = np.zeros((patch_cols // GROUP, 2, GROUP, HALF, 8, patch_cols), np.float32)
    for patch in range(patch_cols):
        at, j = divmod(patch, GROUP)
        second[at, 0, j, :, :7, patch] = weight[:, None] * cosine(k2[:, None] * shift)
        second[at, 1, j, :, :7, patch] = -weight[:, None] * sine(k2[:, None] * shift)
    second = second.reshape(patch_cols * PATCH, 8 * patch_cols)
    direct = np.zeros((lanes.size, 8, patch_cols), np.float32)
    direct[lanes, :7, lanes % patch_cols] = 1.0 / PATCH
    second = np.concatenate([second, direct.reshape(lanes.size, -1)], 0)
    return [t.astype(ml_dtypes.bfloat16) for t in (col, zero, row, row0, first, second)]


def dot(a, b):
    return jnp.dot(a, b, preferred_element_type=f32)


def whitened(now, old):
    now, old = now.astype(f32), old.astype(f32)
    now_real, now_imag = now[:PATCH], now[PATCH:]
    old_real, old_imag = old[:PATCH], old[PATCH:]
    cross_real = now_real * old_real + now_imag * old_imag
    cross_imag = now_imag * old_real - now_real * old_imag
    inverse = lax.rsqrt(
        cross_real * cross_real + cross_imag * cross_imag + whiten_floor * whiten_floor
    )
    return jnp.concatenate([cross_real * inverse, cross_imag * inverse], 0).astype(bf16)


def section_step(load, tabs, spec, spec0, sums, base, mode, early=None, early0=None):
    col, zero, row, row0, first = [t[...] for t in tabs]
    patch_rows, unused, width = spec.shape
    chunks = width // SIDE
    lanes = spec0.shape[1]
    patch_cols = lanes // patch_rows
    upper = patch_rows // 2
    totals = None
    for at in range(chunks):
        x = load(at)
        part = dot(x, zero[at * CHUNK:(at + 1) * CHUNK])
        totals = part if totals is None else totals + part
        halves = [
            dot(x[:, h * CHUNK // 2:(h + 1) * CHUNK // 2], col).astype(bf16) for h in range(2)
        ]
        real = jnp.concatenate([h[:, :SIDE // 2] for h in halves], 1)
        imag = jnp.concatenate([h[:, SIDE // 2:] for h in halves], 1)
        here = slice(at * SIDE, (at + 1) * SIDE)
        for a in range(patch_rows):
            part = slice(a * PATCH, (a + 1) * PATCH)
            now = dot(row, jnp.concatenate([real[part], imag[part]], 0)).astype(bf16)
            if mode != "first":
                if mode == "edge" and a < upper:
                    prod = whitened(early[a, :, here], now)
                else:
                    prod = whitened(now, spec[a, :, here])
                half = dot(first, prod)
                rows = pl.ds(base + a * 8, 8)
                sums[rows, at * CHUNK:at * CHUNK + SIDE] = half[:8]
                sums[rows, at * CHUNK + SIDE:(at + 1) * CHUNK] = half[8:]
            if mode != "edge":
                spec[a, :, here] = now
            if mode == "first" and a < upper:
                early[a, :, here] = now
    lane = lax.broadcasted_iota(jnp.int32, (2 * PATCH, lanes), 1) // patch_cols
    packed = jnp.zeros((PATCH, lanes), f32)
    for a in range(patch_rows):
        packed = jnp.where(lane[:PATCH] == a, totals[a * PATCH:(a + 1) * PATCH], packed)
    now = dot(row0, packed.astype(bf16)).astype(bf16)
    if mode != "first":
        if mode == "edge":
            got = now.astype(f32)
            later = jnp.where(lane < upper, early0[...].astype(f32), got)
            before = jnp.where(lane < upper, got, spec0[...].astype(f32))
        else:
            later, before = now, spec0[...]
        half = dot(first, whitened(later, before))[:8]
        for a in range(patch_rows):
            sums[pl.ds(base + a * 8, 8), chunks * CHUNK:] = jnp.where(lane[:8] == a, half, 0.0)
    if mode != "edge":
        spec0[...] = now
    if mode == "first":
        early0[...] = now


def pick(sums, second, peaks, patch_cols):
    corr = dot(sums.astype(bf16), second)
    count = corr.shape[0] // 8
    width = corr.shape[1]
    corr = corr.reshape(count, 8, width)
    p1, p2 = peaks[0], peaks[1]
    sub = lax.broadcasted_iota(jnp.int32, (count, 8, width), 1).astype(f32) - 3.0
    shift = lax.broadcasted_iota(jnp.int32, (count, width), 1) // patch_cols
    shift = shift.astype(f32) - 3.0
    p1_all = jnp.broadcast_to(p1[:, None, :], (count, 8, width))
    at1 = [jnp.sum(jnp.where(sub == p1_all + d, corr, 0.0), 1) for d in (-1.0, 0.0, 1.0)]

    def fold(values, d):
        values = jnp.where(shift == p2 + d, values, 0.0)
        reach = width // 2
        while reach >= patch_cols:
            values = values + pltpu.roll(values, reach, 1)
            reach //= 2
        return values

    center = fold(at1[1], 0.0)

    def step(low, high):
        return (low - high) / (2.0 * jnp.maximum(jnp.abs(low - 2.0 * center + high), 1.0))

    row_flow = p1 + step(fold(at1[0], 0.0), fold(at1[2], 0.0))
    col_flow = p2 + step(fold(at1[1], -1.0), fold(at1[1], 1.0))
    return row_flow, col_flow


def packed_rows(flow, patch_rows, patch_cols):
    lanes = patch_rows * patch_cols
    flow = flow[:, :lanes].reshape(-1, patch_rows, lanes)
    lane = lax.broadcasted_iota(jnp.int32, flow.shape, 2) // patch_cols
    own = lax.broadcasted_iota(jnp.int32, flow.shape, 1)
    return jnp.sum(jnp.where(lane == own, flow, 0.0), 1)


def kernel(
    sizes, pixels, inner_peaks, top_peaks, low_peaks, weight,
    col_in, zero_in, row_in, row0_in, first_in, second_in,
    out,
    col, zero, row, row0, first, second,
    pix, edge, next_low, spec, spec0, early, early0, sums,
    message, edge_message, inbox, edge_inbox, flows, weights, state, speed,
    pix_sem, tab_sem, edge_send, edge_recv, msg_send, msg_recv, last_send, last_recv,
):
    size_x, size_y, size_s = sizes
    total = size_x * size_y * size_s
    my_x, my_y, my_s = lax.axis_index("gx"), lax.axis_index("gy"), lax.axis_index("sa")
    me = (my_x * size_y + my_y) * size_s + my_s
    count, height, width = pixels.shape
    patch_rows = spec.shape[0]
    lanes = spec0.shape[1]
    patch_cols = lanes // patch_rows
    upper = patch_rows // 2

    def place(i):
        there = lax.rem(me + i, total)
        return there // (size_y * size_s), lax.rem(there // size_s, size_y), lax.rem(there, size_s)

    barrier = pltpu.get_barrier_semaphore()

    @pl.loop(1, total)
    def _(i):
        pl.semaphore_signal(barrier, inc=1, device_id=place(i), device_id_type=MESH)

    pix_copies = [
        pltpu.make_async_copy(pixels.at[s], pix.at[s], pix_sem.at[s]) for s in range(count)
    ]
    tab_copies = [
        pltpu.make_async_copy(a, b, tab_sem.at[i])
        for i, (a, b) in enumerate(
            zip((col_in, zero_in, row_in, row0_in, first_in, second_in),
                (col, zero, row, row0, first, second))
        )
    ]
    pix_copies[0].start()
    for c in tab_copies[:5]:
        c.start()
    for c in pix_copies[1:]:
        c.start()
    tab_copies[5].start()

    half = height // 2
    ahead = pltpu.make_async_remote_copy(
        src_ref=pixels.at[count - 1, pl.ds(0, half)],
        dst_ref=edge.at[pl.ds(0, half)],
        send_sem=edge_send.at[0],
        recv_sem=edge_recv.at[0],
        device_id=(my_x, my_y, lax.rem(my_s + 1, size_s)),
        device_id_type=MESH,
    )
    back_to = (my_x, my_y, lax.rem(my_s + size_s - 1, size_s))
    back = pltpu.make_async_remote_copy(
        src_ref=pixels.at[0, pl.ds(half, half)],
        dst_ref=edge.at[pl.ds(half, half)],
        send_sem=edge_send.at[1],
        recv_sem=edge_recv.at[1],
        device_id=back_to,
        device_id_type=MESH,
    )
    peak_copy = pltpu.make_async_remote_copy(
        src_ref=low_peaks,
        dst_ref=next_low,
        send_sem=edge_send.at[2],
        recv_sem=edge_recv.at[2],
        device_id=back_to,
        device_id_type=MESH,
    )
    pl.semaphore_wait(barrier, total - 1)

    @pl.when(my_s < size_s - 1)
    def _():
        ahead.start()

    @pl.when(my_s > 0)
    def _():
        back.start()

    peak_copy.start()

    @pl.when(my_s == 0)
    def _():
        edge[:half] = jnp.zeros((half, width), bf16)

    @pl.when(my_s == size_s - 1)
    def _():
        edge[half:] = jnp.zeros((half, width), bf16)

    tabs = (col, zero, row, row0, first)
    for c in tab_copies[:5]:
        c.wait()
    for s in range(count):
        pix_copies[s].wait()
        if s == 0:
            section_step(
                lambda at: pix[0, :, at * CHUNK:(at + 1) * CHUNK],
                tabs, spec, spec0, sums, 0, "first", early, early0,
            )
    tab_copies[5].wait()

    @pl.loop(1, count)
    def _(s):
        section_step(
            lambda at: pix[s, :, at * CHUNK:(at + 1) * CHUNK],
            tabs, spec, spec0, sums, pl.multiple_of((s - 1) * patch_rows * 8, 8), "next",
        )

    inner = pick(sums[...], second[...], inner_peaks, patch_cols)
    for c in range(2):
        message[c, :1] = jnp.zeros((1, lanes), f32)
        message[c, 1:] = packed_rows(inner[c], patch_rows, patch_cols)
    message[2] = weight[...]
    inbox[my_x, my_y, my_s] = message[...]

    def sender(i, source, box, send, recv):
        return pltpu.make_async_remote_copy(
            src_ref=source,
            dst_ref=box.at[my_x, my_y, my_s],
            send_sem=send.at[i],
            recv_sem=recv.at[total - i],
            device_id=place(i),
            device_id_type=MESH,
        )

    def arrival(i, source, box, send, recv):
        x, y, s = place(i)
        return pltpu.make_async_remote_copy(
            src_ref=source,
            dst_ref=box.at[x, y, s],
            send_sem=send.at[i],
            recv_sem=recv.at[i],
            device_id=place(i),
            device_id_type=MESH,
        )

    inner_args = (message, inbox, msg_send, msg_recv)
    last_args = (edge_message, edge_inbox, last_send, last_recv)

    @pl.loop(1, total)
    def _(i):
        sender(i, *inner_args).start()

    @pl.when(my_s > 0)
    def _():
        ahead.wait_recv()

    @pl.when(my_s < size_s - 1)
    def _():
        back.wait_recv()

    peak_copy.wait_recv()
    section_step(
        lambda at: edge[:, at * CHUNK:(at + 1) * CHUNK],
        tabs, spec, spec0, sums, 0, "edge", early, early0,
    )
    edge_peaks = [jnp.concatenate([top_peaks[c], next_low[c]], 0) for c in range(2)]
    outer = pick(sums[:patch_rows * 8], second[...], edge_peaks, patch_cols)
    for c in range(2):
        edge_message[c:c + 1] = packed_rows(outer[c], patch_rows, patch_cols)
    edge_inbox[my_x, my_y, my_s] = edge_message[...]

    @pl.loop(1, total)
    def _(i):
        sender(i, *last_args).start()

    @pl.loop(1, total)
    def _(i):
        arrival(i, *inner_args).wait_recv()

    @pl.loop(1, total)
    def _(i):
        arrival(i, *last_args).wait_recv()

    sections = size_s * count
    total_rows, total_cols = size_y * patch_rows, size_x * patch_cols
    sub = lax.broadcasted_iota(jnp.int32, (sections, lanes), 0)
    lane = lax.broadcasted_iota(jnp.int32, (sections, lanes), 1)
    for y in range(size_y):
        for c in range(3):
            rows = [None] * patch_rows
            for x in range(size_x):
                block = jnp.concatenate([inbox[x, y, s, c] for s in range(size_s)], 0)
                if c < 2:
                    for s in range(size_s):
                        own = edge_inbox[x, y, s, c:c + 1]
                        before = edge_inbox[x, y, (s - 1) % size_s, c:c + 1]
                        begin = jnp.where(lane[:1] < upper * patch_cols, own, before)
                        block = jnp.where(sub == s * count, begin, block)
                for a in range(patch_rows):
                    turn = (x - a) * patch_cols % lanes
                    moved = pltpu.roll(block, turn, 1) if turn else block
                    if rows[a] is None:
                        rows[a] = moved
                    else:
                        rows[a] = jnp.where(lane // patch_cols == x, moved, rows[a])
            for a in range(patch_rows):
                if c < 2:
                    flows[c, y * patch_rows + a] = rows[a]
                else:
                    weights[y * patch_rows + a] = rows[a]

    def up(values):
        moved = pltpu.roll(values, sections - 1, values.ndim - 2)
        at = lax.broadcasted_iota(jnp.int32, values.shape, values.ndim - 2)
        return jnp.where(at == sections - 1, 0.0, moved)

    def down(values, by=1):
        moved = pltpu.roll(values, by, values.ndim - 2)
        at = lax.broadcasted_iota(jnp.int32, values.shape, values.ndim - 2)
        return jnp.where(at < by, 0.0, moved)

    running = flows[...]
    by = 1
    while by < sections:
        running = running + down(running, by)
        by *= 2
    state[0] = running
    speed[...] = jnp.zeros_like(running)
    first_col, last_col = lane == 0, lane == total_cols - 1
    ends = first_col.astype(f32) + last_col.astype(f32)

    for t in range(RELAX):
        now_at, then_at = t % 2, (t + 1) % 2

        @pl.loop(0, 2)
        def _(c):
            for r in range(total_rows):
                now = state[now_at, c, r]
                flow, w = flows[c, r], weights[r]
                around = jnp.where(first_col, 0.0, pltpu.roll(now, 1, 1)) + jnp.where(
                    last_col, 0.0, pltpu.roll(now, total_cols - 1, 1)
                )
                degree = 4.0 - ends
                if r > 0:
                    around = around + state[now_at, c, r - 1]
                else:
                    degree = degree - 1.0
                if r < total_rows - 1:
                    around = around + state[now_at, c, r + 1]
                else:
                    degree = degree - 1.0
                here_term = w * (now - down(now) - flow)
                next_term = up(here_term)
                gradient = spring_plane * (degree * now - around) + spring_stack * (
                    here_term - next_term
                )
                velocity = damping * speed[c, r] - step_size * gradient
                speed[c, r] = velocity
                state[then_at, c, r] = now + velocity

    where_s = my_s * count
    for field in range(2):
        for c in range(2):
            for a in range(patch_rows):
                r = my_y * patch_rows + a
                if field == 0:
                    values = flows[c, r, pl.ds(where_s, count)]
                else:
                    values = state[RELAX % 2, c, r, pl.ds(where_s, count)]
                mine = values
                for x in range(1, size_x):
                    moved = pltpu.roll(values, lanes - x * patch_cols, 1)
                    mine = jnp.where(my_x == x, moved, mine)
                out[field, c, a] = mine[:, :patch_cols]

    @pl.when(my_s < size_s - 1)
    def _():
        ahead.wait_send()

    @pl.when(my_s > 0)
    def _():
        back.wait_send()

    peak_copy.wait_send()

    @pl.loop(1, total)
    def _(i):
        sender(i, *inner_args).wait_send()

    @pl.loop(1, total)
    def _(i):
        sender(i, *last_args).wait_send()


def per_device(pixels, peak_offsets, validity):
    count, height, width = pixels.shape
    patch_rows, patch_cols = peak_offsets.shape[2:]
    lanes = patch_rows * patch_cols
    upper = patch_rows // 2
    sizes = tuple(lax.axis_size(axis) for axis in ("gx", "gy", "sa"))
    size_x, size_y, size_s = sizes
    total = math.prod(sizes)
    sections = size_s * count
    total_rows = size_y * patch_rows
    peaks = jnp.tile(peak_offsets.astype(f32), (1, 1, 1, 8))
    inner_peaks = jnp.transpose(peaks[1:], (1, 0, 2, 3)).reshape(2, -1, 8 * patch_cols)
    weight = validity.astype(f32).reshape(count, lanes)
    tabs = [jnp.asarray(t) for t in tables(patch_rows, patch_cols)]
    vmem = pl.BlockSpec(memory_space=pltpu.VMEM)
    anywhere = pl.BlockSpec(memory_space=pl.ANY)
    dma = pltpu.SemaphoreType.DMA
    plane = (sections, lanes)
    out = pl.pallas_call(
        functools.partial(kernel, sizes),
        in_specs=[anywhere] + [vmem] * 4 + [anywhere] * 6,
        out_specs=vmem,
        out_shape=jax.ShapeDtypeStruct((2, 2, patch_rows, count, patch_cols), f32),
        scratch_shapes=[pltpu.VMEM(t.shape, bf16) for t in tabs]
        + [
            pltpu.VMEM(pixels.shape, bf16),
            pltpu.VMEM((height, width), bf16),
            pltpu.VMEM((2, patch_rows - upper, 8 * patch_cols), f32),
            pltpu.VMEM((patch_rows, 2 * PATCH, patch_cols * HALF), bf16),
            pltpu.VMEM((2 * PATCH, lanes), bf16),
            pltpu.VMEM((upper, 2 * PATCH, patch_cols * HALF), bf16),
            pltpu.VMEM((2 * PATCH, lanes), bf16),
            pltpu.VMEM(((count - 1) * patch_rows * 8, patch_cols * PATCH + lanes), f32),
            pltpu.VMEM((3, count, lanes), f32),
            pltpu.VMEM((2, lanes), f32),
            pltpu.VMEM(sizes + (3, count, lanes), f32),
            pltpu.VMEM(sizes + (2, lanes), f32),
            pltpu.VMEM((2, total_rows) + plane, f32),
            pltpu.VMEM((total_rows,) + plane, f32),
            pltpu.VMEM((2, 2, total_rows) + plane, f32),
            pltpu.VMEM((2, total_rows) + plane, f32),
            dma((count,)),
            dma((6,)),
            dma((3,)),
            dma((3,)),
            dma((total,)),
            dma((total,)),
            dma((total,)),
            dma((total,)),
        ],
        compiler_params=pltpu.CompilerParams(
            collective_id=0, has_side_effects=True, vmem_limit_bytes=56 * 1024 * 1024
        ),
        name="align",
    )(pixels, inner_peaks, peaks[0, :, :upper], peaks[0, :, upper:], weight, *tabs)
    fields = jnp.transpose(out, (0, 3, 1, 2, 4))
    return fields[0], fields[1]


def solution(mesh):
    return jax.shard_map(
        per_device,
        mesh=mesh,
        in_specs=(P("sa", "gy", "gx"), P("sa", None, "gy", "gx"), P("sa", "gy", "gx")),
        out_specs=(P("sa", None, "gy", "gx"), P("sa", None, "gy", "gx")),
        check_vma=False,
    )
```

time: 64.6 us -> 43.1 us (0.67)
  local copies, waits for them, and re-layouts: 15.8 us -> 4.09 us
  starting transfers between devices: 10.9 us -> 0 us
  Pallas kernels: 34.2 us -> 36.5 us
  other arithmetic: 2.11 us -> 1.42 us
    ppermute x3 -> x0, starting transfers between devices: 10.9 us -> none  [the longest x1 5.05 us: per_device(): next_peaks = lax.ppermute(peaks[0, :, half_rows:], 'sa', ring)]
    unnamed x31 -> x2, local copies, waits for them, and re-layouts: 10.4 us -> 1.22 us
    pallas_call x4 -> x1, Pallas kernels: 34.2 us -> 36.5 us  [per_device(): pl.pallas_call(functools.partial(kernel, sizes), in_specs=[anywhere] + [v...]
    slice x10 -> x2, local copies, waits for them, and re-layouts: 2.26 us -> 0.01 us  [per_device(): peaks[1:]]
    squeeze x2, local copies, waits for them, and re-layouts: 0.01 us -> 1.34 us  [the longest x1 0.74 us: per_device(): return (fields[0], fields[1])]
    concatenate x3 -> x0, other arithmetic: 1.06 us -> none  [the longest x1 1.04 us: gather(): return jnp.roll(got, me, axis=0)]
    dynamic_slice x3 -> x0, local copies, waits for them, and re-layouts: 0.84 us -> none  [the longest x1 0.69 us: per_device(): lax.dynamic_slice(final, starts, shape)]
    convert_element_type x2, other arithmetic: 0.73 us -> 1.42 us  [the longest x1 0.72 us: per_device(): peaks = jnp.tile(peak_offsets.astype(f32), (1, 1, 1, 8))]
  transfers between devices with their start and end apart: 3 -> 0, of which waited for: 0 -> 0; matrix products, arithmetic and copies ran while one was open for 4% -> 0% of each run, Pallas kernels for 24% -> 0%
where the time goes in v2:
time: 43.1 us; the launch traced here: 42.7 us
  Pallas kernels  36.5 us (85%)
  local copies, waits for them, and re-layouts  4.09 us (9%)
  other arithmetic  1.42 us (3%)
  between operations  0.66 us (2%)
    pallas_call x1, Pallas kernels, per_device(): pl.pallas_call(functools.partial(kernel, sizes), in_specs=[anywhere] + [v...  36.5 us
    unnamed x2, local copies, waits for them, and re-layouts  1.22 us

profile of v2, /device:TPU:0, one launch (start us, length us, event | category | flops | bytes accessed | tf_op | source)
XLA Modules:
  0.0 42.7 jit_solution(2168730855302683821)
XLA Ops:
  0.6 0.7 %convert_element_type.6 = f32[4,2,4,32]{3,2,1,0:T(4,128)S(1)} convert(s32[4,2,4,32]{3,2,1,0:T(4,128)} %param.10) | non-fusion elementwise | flops 1024 | bytes 8192 | tf_op jit(solution)/shard_map/convert_element_type | solution.py:480
  1.4 0.1 tile.16
  1.5 0.6 %slice_bitcast_fusion.2 = (f32[2,2,256]{2,1,0:T(2,128)}, f32[2,2,256]{2,1,0:T(2,128)}) fusion(f32[4,2,4,256]{3,2,1,0:T(4,128)S(1)} %tile.16), kind=kLoop, calls=%fused_computation.2 | loop fusion | bytes 16384 | tf_op jit(solution)/shard_map/squeeze | solution.py:524
  2.1 0.1 tile.14
  2.2 0.6 %copy.15.inner_peaks = f32[2,12,256]{2,1,0:T(8,128)} copy(f32[2,12,256]{2,0,1:T(2,128)S(1)} %bitcast.19) | data formatting | bytes 49152 | tf_op jit(solution)/shard_map/reshape | solution.py:481
  2.8 0.7 %convert_element_type.7 = f32[4,4,32]{2,1,0:T(4,128)S(1)} convert(s32[4,4,32]{2,1,0:T(4,128)} %param.11) | non-fusion elementwise | flops 512 | bytes 4096 | tf_op jit(solution)/shard_map/convert_element_type | solution.py:482
  3.5 0.7 %reshape.17.weight = f32[4,128]{1,0:T(4,128)} reshape(f32[4,4,32]{2,1,0:T(4,128)S(1)} %convert_element_type.7) | data formatting | bytes 4096 | tf_op jit(solution)/shard_map/reshape | solution.py:482
  4.2 36.5 %align.1 = f32[2,2,4,4,32]{4,3,2,1,0:T(4,128)} custom-call(bf16[4,256,2048]{2,1,0:T(8,128)(2,1)} %pixels.1, f32[2,12,256]{2,1,0:T(8,128)} %copy.15.inner_peaks, f32[2,2,256]{2,1,0:T(2,128)} %get-tuple-element.9.top_peaks, f32[2,2,256]{2,1,0:T(2,128)} %get-tuple-element.8.low_peaks, f32[4,128]{1,0:T(4,128)} %reshape.17.weight, ...), custom_call_target="tpu_custom_call" | custom-call | tf_op jit(solution)/shard_map/align/pallas_call | solution.py:488
  40.7 0.7 %slice_bitcast_fusion = (f32[4,2,4,32]{3,0,2,1:T(4,128)S(1)}, f32[4,2,4,32]{3,0,2,1:T(4,128)S(1)}) fusion(f32[2,4,2,4,32]{4,1,3,2,0:T(4,128)} %bitcast.18), kind=kLoop, calls=%fused_computation | loop fusion | bytes 16384 | tf_op jit(solution)/shard_map/squeeze | solution.py:526
  41.4 0.6 %copy.16 = f32[4,2,4,32]{3,2,1,0:T(4,128)} copy(f32[4,2,4,32]{3,0,2,1:T(4,128)S(1)} %get-tuple-element.7) | data formatting | bytes 8192
  42.0 0.6 %copy.17 = f32[4,2,4,32]{3,2,1,0:T(4,128)} copy(f32[4,2,4,32]{3,0,2,1:T(4,128)S(1)} %get-tuple-element.6) | data formatting | bytes 8192
  (4 shorter events, 0.0 us)

commit v3 on v2

--- a/solution.py
+++ b/solution.py
@@ -13,9 +13,6 @@
 PATCH = 64
 HALF = PATCH // 2
 RELAX = 8
-GROUP = 8
-CHUNK = GROUP * PATCH
-SIDE = GROUP * HALF
 
 spring_plane = 0.5
 spring_stack = 1.0
@@ -58,11 +55,10 @@
     first[:7] = np.concatenate([cosine(shift[:, None] * y), -sine(shift[:, None] * y)], 1)
     first[8:15] = np.concatenate([sine(shift[:, None] * y), cosine(shift[:, None] * y)], 1)
     weight = np.where(k2 == HALF, 1.0, 2.0) / PATCH
-    second = np.zeros((patch_cols // GROUP, 2, GROUP, HALF, 8, patch_cols), np.float32)
+    second = np.zeros((2, patch_cols, HALF, 8, patch_cols), np.float32)
     for patch in range(patch_cols):
-        at, j = divmod(patch, GROUP)
-        second[at, 0, j, :, :7, patch] = weight[:, None] * cosine(k2[:, None] * shift)
-        second[at, 1, j, :, :7, patch] = -weight[:, None] * sine(k2[:, None] * shift)
+        second[0, patch, :, :7, patch] = weight[:, None] * cosine(k2[:, None] * shift)
+        second[1, patch, :, :7, patch] = -weight[:, None] * sine(k2[:, None] * shift)
     second = second.reshape(patch_cols * PATCH, 8 * patch_cols)
     direct = np.zeros((lanes.size, 8, patch_cols), np.float32)
     direct[lanes, :7, lanes % patch_cols] = 1.0 / PATCH
@@ -86,40 +82,36 @@
     return jnp.concatenate([cross_real * inverse, cross_imag * inverse], 0).astype(bf16)
 
 
-def section_step(load, tabs, spec, spec0, sums, base, mode, early=None, early0=None):
+def section_step(x, tabs, spec, spec0, cols, sums, base, mode, early=None, early0=None):
     col, zero, row, row0, first = [t[...] for t in tabs]
     patch_rows, unused, width = spec.shape
-    chunks = width // SIDE
     lanes = spec0.shape[1]
     patch_cols = lanes // patch_rows
     upper = patch_rows // 2
-    totals = None
-    for at in range(chunks):
-        x = load(at)
-        part = dot(x, zero[at * CHUNK:(at + 1) * CHUNK])
-        totals = part if totals is None else totals + part
-        halves = [
-            dot(x[:, h * CHUNK // 2:(h + 1) * CHUNK // 2], col).astype(bf16) for h in range(2)
-        ]
-        real = jnp.concatenate([h[:, :SIDE // 2] for h in halves], 1)
-        imag = jnp.concatenate([h[:, SIDE // 2:] for h in halves], 1)
-        here = slice(at * SIDE, (at + 1) * SIDE)
+    group, out = 4 * PATCH, 4 * HALF
+    for at in range(width // out):
+        part = dot(x[:, at * group:(at + 1) * group], col).astype(bf16)
+        here = slice(at * out, (at + 1) * out)
         for a in range(patch_rows):
-            part = slice(a * PATCH, (a + 1) * PATCH)
-            now = dot(row, jnp.concatenate([real[part], imag[part]], 0)).astype(bf16)
-            if mode != "first":
-                if mode == "edge" and a < upper:
-                    prod = whitened(early[a, :, here], now)
-                else:
-                    prod = whitened(now, spec[a, :, here])
-                half = dot(first, prod)
-                rows = pl.ds(base + a * 8, 8)
-                sums[rows, at * CHUNK:at * CHUNK + SIDE] = half[:8]
-                sums[rows, at * CHUNK + SIDE:(at + 1) * CHUNK] = half[8:]
-            if mode != "edge":
-                spec[a, :, here] = now
-            if mode == "first" and a < upper:
-                early[a, :, here] = now
+            rows = slice(a * PATCH, (a + 1) * PATCH)
+            cols[a, :PATCH, here] = part[rows, :out]
+            cols[a, PATCH:, here] = part[rows, out:]
+    totals = dot(x[...], zero)
+    for a in range(patch_rows):
+        now = dot(row, cols[a]).astype(bf16)
+        if mode != "first":
+            if mode == "edge" and a < upper:
+                prod = whitened(early[a], now)
+            else:
+                prod = whitened(now, spec[a])
+            half = dot(first, prod)
+            rows = pl.ds(base + a * 8, 8)
+            sums[rows, :width] = half[:8]
+            sums[rows, width:2 * width] = half[8:]
+        if mode != "edge":
+            spec[a] = now
+        if mode == "first" and a < upper:
+            early[a] = now
     lane = lax.broadcasted_iota(jnp.int32, (2 * PATCH, lanes), 1) // patch_cols
     packed = jnp.zeros((PATCH, lanes), f32)
     for a in range(patch_rows):
@@ -134,7 +126,7 @@
             later, before = now, spec0[...]
         half = dot(first, whitened(later, before))[:8]
         for a in range(patch_rows):
-            sums[pl.ds(base + a * 8, 8), chunks * CHUNK:] = jnp.where(lane[:8] == a, half, 0.0)
+            sums[pl.ds(base + a * 8, 8), 2 * width:] = jnp.where(lane[:8] == a, half, 0.0)
     if mode != "edge":
         spec0[...] = now
     if mode == "first":
@@ -180,11 +172,11 @@
 
 
 def kernel(
-    sizes, pixels, inner_peaks, top_peaks, low_peaks, weight,
+    sizes, pixels, peaks, validity,
     col_in, zero_in, row_in, row0_in, first_in, second_in,
-    out,
+    flow_out, mesh_out,
     col, zero, row, row0, first, second,
-    pix, edge, next_low, spec, spec0, early, early0, sums,
+    pix, edge, next_peaks, spec, spec0, early, early0, cols, sums,
     message, edge_message, inbox, edge_inbox, flows, weights, state, speed,
     pix_sem, tab_sem, edge_send, edge_recv, msg_send, msg_recv, last_send, last_recv,
 ):
@@ -198,15 +190,14 @@
     patch_cols = lanes // patch_rows
     upper = patch_rows // 2
 
-    def place(i):
-        there = lax.rem(me + i, total)
-        return there // (size_y * size_s), lax.rem(there // size_s, size_y), lax.rem(there, size_s)
+    at_x = [lax.rem(my_x + d, size_x) for d in range(size_x)]
+    at_y = [lax.rem(my_y + d, size_y) for d in range(size_y)]
+    at_s = [lax.rem(my_s + d, size_s) for d in range(size_s)]
+    others = [(x, y, s) for s in at_s for x in at_x for y in at_y][1:]
 
     barrier = pltpu.get_barrier_semaphore()
-
-    @pl.loop(1, total)
-    def _(i):
-        pl.semaphore_signal(barrier, inc=1, device_id=place(i), device_id_type=MESH)
+    for device in others:
+        pl.semaphore_signal(barrier, inc=1, device_id=device, device_id_type=MESH)
 
     pix_copies = [
         pltpu.make_async_copy(pixels.at[s], pix.at[s], pix_sem.at[s]) for s in range(count)
@@ -244,8 +235,8 @@
         device_id_type=MESH,
     )
     peak_copy = pltpu.make_async_remote_copy(
-        src_ref=low_peaks,
-        dst_ref=next_low,
+        src_ref=peaks.at[0],
+        dst_ref=next_peaks,
         send_sem=edge_send.at[2],
         recv_sem=edge_recv.at[2],
         device_id=back_to,
@@ -278,52 +269,57 @@
         pix_copies[s].wait()
         if s == 0:
             section_step(
-                lambda at: pix[0, :, at * CHUNK:(at + 1) * CHUNK],
-                tabs, spec, spec0, sums, 0, "first", early, early0,
+                pix.at[0], tabs, spec, spec0, cols, sums, 0, "first", early, early0
             )
     tab_copies[5].wait()
 
     @pl.loop(1, count)
     def _(s):
         section_step(
-            lambda at: pix[s, :, at * CHUNK:(at + 1) * CHUNK],
-            tabs, spec, spec0, sums, pl.multiple_of((s - 1) * patch_rows * 8, 8), "next",
+            pix.at[s], tabs, spec, spec0, cols, sums,
+            pl.multiple_of((s - 1) * patch_rows * 8, 8), "next",
         )
 
+    repeat = (patch_cols, 8 * patch_cols)
+    spread = (
+        lax.broadcasted_iota(jnp.int32, repeat, 1) % patch_cols
+        == lax.broadcasted_iota(jnp.int32, repeat, 0)
+    ).astype(f32).astype(bf16)
+
+    def repeated(blocks):
+        return dot(jnp.concatenate([b.astype(f32) for b in blocks], 0).astype(bf16), spread)
+
+    inner_peaks = [repeated([peaks[s, c] for s in range(1, count)]) for c in range(2)]
+    weight = packed_rows(repeated([validity[s] for s in range(count)]), patch_rows, patch_cols)
     inner = pick(sums[...], second[...], inner_peaks, patch_cols)
     for c in range(2):
         message[c, :1] = jnp.zeros((1, lanes), f32)
         message[c, 1:] = packed_rows(inner[c], patch_rows, patch_cols)
-    message[2] = weight[...]
-    inbox[my_x, my_y, my_s] = message[...]
-
-    def sender(i, source, box, send, recv):
+    message[2] = weight
+    inbox[me] = message[...]
+
+    def push(source, box, send, recv):
+        for device in others:
+            pltpu.make_async_remote_copy(
+                src_ref=source,
+                dst_ref=box.at[me],
+                send_sem=send,
+                recv_sem=recv,
+                device_id=device,
+                device_id_type=MESH,
+            ).start()
+
+    def every(box, send, recv):
         return pltpu.make_async_remote_copy(
-            src_ref=source,
-            dst_ref=box.at[my_x, my_y, my_s],
-            send_sem=send.at[i],
-            recv_sem=recv.at[total - i],
-            device_id=place(i),
+            src_ref=box.at[pl.ds(0, total - 1)],
+            dst_ref=box.at[pl.ds(0, total - 1)],
+            send_sem=send,
+            recv_sem=recv,
+            device_id=others[0],
             device_id_type=MESH,
         )
 
-    def arrival(i, source, box, send, recv):
-        x, y, s = place(i)
-        return pltpu.make_async_remote_copy(
-            src_ref=source,
-            dst_ref=box.at[x, y, s],
-            send_sem=send.at[i],
-            recv_sem=recv.at[i],
-            device_id=place(i),
-            device_id_type=MESH,
-        )
-
-    inner_args = (message, inbox, msg_send, msg_recv)
-    last_args = (edge_message, edge_inbox, last_send, last_recv)
-
-    @pl.loop(1, total)
-    def _(i):
-        sender(i, *inner_args).start()
+    push(message, inbox, msg_send, msg_recv)
 
     @pl.when(my_s > 0)
     def _():
@@ -335,26 +331,16 @@
 
     peak_copy.wait_recv()
     section_step(
-        lambda at: edge[:, at * CHUNK:(at + 1) * CHUNK],
-        tabs, spec, spec0, sums, 0, "edge", early, early0,
+        edge, tabs, spec, spec0, cols, sums, 0, "edge", early, early0
     )
-    edge_peaks = [jnp.concatenate([top_peaks[c], next_low[c]], 0) for c in range(2)]
+    edge_peaks = [repeated([peaks[0, c, :upper], next_peaks[c, upper:]]) for c in range(2)]
     outer = pick(sums[:patch_rows * 8], second[...], edge_peaks, patch_cols)
     for c in range(2):
         edge_message[c:c + 1] = packed_rows(outer[c], patch_rows, patch_cols)
-    edge_inbox[my_x, my_y, my_s] = edge_message[...]
-
-    @pl.loop(1, total)
-    def _(i):
-        sender(i, *last_args).start()
-
-    @pl.loop(1, total)
-    def _(i):
-        arrival(i, *inner_args).wait_recv()
-
-    @pl.loop(1, total)
-    def _(i):
-        arrival(i, *last_args).wait_recv()
+    edge_inbox[me] = edge_message[...]
+    push(edge_message, edge_inbox, last_send, last_recv)
+    every(inbox, msg_send, msg_recv).wait_recv()
+    every(edge_inbox, last_send, last_recv).wait_recv()
 
     sections = size_s * count
     total_rows, total_cols = size_y * patch_rows, size_x * patch_cols
@@ -364,11 +350,12 @@
         for c in range(3):
             rows = [None] * patch_rows
             for x in range(size_x):
-                block = jnp.concatenate([inbox[x, y, s, c] for s in range(size_s)], 0)
+                at = (x * size_y + y) * size_s
+                block = jnp.concatenate([inbox[at + s, c] for s in range(size_s)], 0)
                 if c < 2:
                     for s in range(size_s):
-                        own = edge_inbox[x, y, s, c:c + 1]
-                        before = edge_inbox[x, y, (s - 1) % size_s, c:c + 1]
+                        own = edge_inbox[at + s, c:c + 1]
+                        before = edge_inbox[at + (s - 1) % size_s, c:c + 1]
                         begin = jnp.where(lane[:1] < upper * patch_cols, own, before)
                         block = jnp.where(sub == s * count, begin, block)
                 for a in range(patch_rows):
@@ -446,7 +433,9 @@
                 for x in range(1, size_x):
                     moved = pltpu.roll(values, lanes - x * patch_cols, 1)
                     mine = jnp.where(my_x == x, moved, mine)
-                out[field, c, a] = mine[:, :patch_cols]
+                out = mesh_out if field else flow_out
+                for s in range(count):
+                    out[s, c, a:a + 1] = mine[s:s + 1, :patch_cols]
 
     @pl.when(my_s < size_s - 1)
     def _():
@@ -458,13 +447,8 @@
 
     peak_copy.wait_send()
 
-    @pl.loop(1, total)
-    def _(i):
-        sender(i, *inner_args).wait_send()
-
-    @pl.loop(1, total)
-    def _(i):
-        sender(i, *last_args).wait_send()
+    every(inbox, msg_send, msg_recv).wait_send()
+    every(edge_inbox, last_send, last_recv).wait_send()
 
 
 def per_device(pixels, peak_offsets, validity):
@@ -477,33 +461,32 @@
     total = math.prod(sizes)
     sections = size_s * count
     total_rows = size_y * patch_rows
-    peaks = jnp.tile(peak_offsets.astype(f32), (1, 1, 1, 8))
-    inner_peaks = jnp.transpose(peaks[1:], (1, 0, 2, 3)).reshape(2, -1, 8 * patch_cols)
-    weight = validity.astype(f32).reshape(count, lanes)
     tabs = [jnp.asarray(t) for t in tables(patch_rows, patch_cols)]
     vmem = pl.BlockSpec(memory_space=pltpu.VMEM)
     anywhere = pl.BlockSpec(memory_space=pl.ANY)
     dma = pltpu.SemaphoreType.DMA
     plane = (sections, lanes)
-    out = pl.pallas_call(
+    shape = jax.ShapeDtypeStruct(peak_offsets.shape, f32)
+    return pl.pallas_call(
         functools.partial(kernel, sizes),
-        in_specs=[anywhere] + [vmem] * 4 + [anywhere] * 6,
-        out_specs=vmem,
-        out_shape=jax.ShapeDtypeStruct((2, 2, patch_rows, count, patch_cols), f32),
+        in_specs=[anywhere] + [vmem] * 2 + [anywhere] * 6,
+        out_specs=(vmem, vmem),
+        out_shape=(shape, shape),
         scratch_shapes=[pltpu.VMEM(t.shape, bf16) for t in tabs]
         + [
             pltpu.VMEM(pixels.shape, bf16),
             pltpu.VMEM((height, width), bf16),
-            pltpu.VMEM((2, patch_rows - upper, 8 * patch_cols), f32),
+            pltpu.VMEM(peak_offsets.shape[1:], jnp.int32),
             pltpu.VMEM((patch_rows, 2 * PATCH, patch_cols * HALF), bf16),
             pltpu.VMEM((2 * PATCH, lanes), bf16),
             pltpu.VMEM((upper, 2 * PATCH, patch_cols * HALF), bf16),
             pltpu.VMEM((2 * PATCH, lanes), bf16),
+            pltpu.VMEM((patch_rows, 2 * PATCH, patch_cols * HALF), bf16),
             pltpu.VMEM(((count - 1) * patch_rows * 8, patch_cols * PATCH + lanes), f32),
             pltpu.VMEM((3, count, lanes), f32),
             pltpu.VMEM((2, lanes), f32),
-            pltpu.VMEM(sizes + (3, count, lanes), f32),
-            pltpu.VMEM(sizes + (2, lanes), f32),
+            pltpu.VMEM((total, 3, count, lanes), f32),
+            pltpu.VMEM((total, 2, lanes), f32),
             pltpu.VMEM((2, total_rows) + plane, f32),
             pltpu.VMEM((total_rows,) + plane, f32),
             pltpu.VMEM((2, 2, total_rows) + plane, f32),
@@ -512,18 +495,16 @@
             dma((6,)),
             dma((3,)),
             dma((3,)),
-            dma((total,)),
-            dma((total,)),
-            dma((total,)),
-            dma((total,)),
+            dma,
+            dma,
+            dma,
+            dma,
         ],
         compiler_params=pltpu.CompilerParams(
             collective_id=0, has_side_effects=True, vmem_limit_bytes=56 * 1024 * 1024
         ),
         name="align",
-    )(pixels, inner_peaks, peaks[0, :, :upper], peaks[0, :, upper:], weight, *tabs)
-    fields = jnp.transpose(out, (0, 3, 1, 2, 4))
-    return fields[0], fields[1]
+    )(pixels, peak_offsets, validity, *tabs)
 
 
 def solution(mesh):

time: 43.1 us -> 35.3 us (0.82)
  Pallas kernels: 36.5 us -> 31.6 us
  local copies, waits for them, and re-layouts: 4.09 us -> 2.65 us
  other arithmetic: 1.42 us -> 0 us
    pallas_call x1, Pallas kernels: 36.5 us -> 31.6 us  [per_device(): pl.pallas_call(functools.partial(kernel, sizes), in_specs=[anywhere] + [v...]
    unnamed x2, local copies, waits for them, and re-layouts: 1.22 us -> 2.65 us
    convert_element_type x2 -> x0, other arithmetic: 1.42 us -> none  [the longest x1 0.72 us: per_device(): peaks = jnp.tile(peak_offsets.astype(f32), (1, 1, 1, 8))]
    squeeze x2 -> x0, local copies, waits for them, and re-layouts: 1.34 us -> none  [the longest x1 0.74 us: per_device(): return (fields[0], fields[1])]
    reshape x2 -> x0, local copies, waits for them, and re-layouts: 1.29 us -> none  [the longest x1 0.68 us: per_device(): weight = validity.astype(f32).reshape(count, lanes)]
where the time goes in v3:
time: 35.3 us; the launch traced here: 34.8 us
  Pallas kernels  31.6 us (90%)
  local copies, waits for them, and re-layouts  2.65 us (8%)
  between operations  0.64 us (2%)
    pallas_call x1, Pallas kernels, per_device(): pl.pallas_call(functools.partial(kernel, sizes), in_specs=[anywhere] + [v...  31.6 us
    unnamed x2, local copies, waits for them, and re-layouts  2.65 us

profile of v3, /device:TPU:0, one launch (start us, length us, event | category | flops | bytes accessed | tf_op | source)
XLA Modules:
  0.0 34.8 jit_solution(3528888290868451774)
XLA Ops:
  0.6 31.6 %align.1 = (f32[4,2,4,32]{3,2,1,0:T(4,128)}, f32[4,2,4,32]{3,2,1,0:T(4,128)}) custom-call(bf16[4,256,2048]{2,1,0:T(8,128)(2,1)} %pixels.1, s32[4,2,4,32]{3,2,1,0:T(4,128)} %peaks.1, s32[4,4,32]{2,1,0:T(4,128)} %validity.1, bf16[256,256]{1,0:T(8,128)(2,1)} %constant.12.clone.col_in, bf16[2048,128]{1,0:T(8,128)(2,1)} %constant.13.clone.zero_in, ...), custom_call_target="tpu_custom_call" | custom-call | tf_op jit(solution)/shard_map/align/pallas_call | solution.py:470
  32.2 1.3 %copy.13 = f32[4,2,4,32]{3,2,1,0:T(4,128)} copy(f32[4,2,4,32]{3,2,1,0:T(4,128)} %get-tuple-element.4) | data formatting | bytes 8192
  33.5 1.3 %copy.14 = f32[4,2,4,32]{3,2,1,0:T(4,128)} copy(f32[4,2,4,32]{3,2,1,0:T(4,128)} %get-tuple-element.5) | data formatting | bytes 8192
